TPU v7x, 32 devices: a whole 2x2x4 slice. The times are simulated.
32 devices in a mesh: blk: 16 (over z, y, core), rep: 2 (over x).
Axes of the slice: x: 2, y: 2, z: 4, core: 2. Of those that a mesh axis runs over, the one named last changes fastest.
Arguments:
- points: float32 [16, 5120], P(None, ('blk', 'rep')), may hold values from -3 to 3
- vectors: float32 [32, 5120], P(None, ('blk', 'rep')), may hold values from -1.2 to 1.2
- lengthscales: float32 [16], replicated, may hold values from 0.6 to 1.6
Outputs:
- product: float32 [32, 5120], P(None, ('blk', 'rep'))
All inputs are finite; a program needn't handle non-finite values.
Results may differ from a plain program's by a relative error of at most 0.0003.
Values sent between devices are 32-bit elements; how exact they have to be, the bound alone decides.
No kernel may reach another device: no remote copies, remote signals or barrier semaphores. Data moves between devices by JAX's collectives and lax.ppermute only.
A program may use at most 64 MiB of HBM per device.

v0:
```python
import functools
import math

import jax
import jax.numpy as jnp
from jax import lax
from jax.experimental import pallas as pl
from jax.experimental.pallas import tpu as pltpu
from jax.sharding import PartitionSpec as P

AXES = ("blk", "rep")
LANES = 128
MIB = 1024 * 1024


def split_blocks(blk, rep):
    pair = 2 if blk % 2 == 0 else 1
    line = blk // pair
    mid = max(d for d in range(1, line + 1) if line % d == 0 and d * d <= line)
    return line // mid, mid, pair, rep


def partner(index, step, size):
    return index ^ step if size & (size - 1) == 0 else (index + step) % size


def permutation(sizes, axis, step):
    far, mid, pair, rep = sizes
    pairs = []
    for target in range(far * mid * pair * rep):
        rest, q = divmod(target, rep)
        rest, p = divmod(rest, pair)
        f, m = divmod(rest, mid)
        if axis == "far":
            f = partner(f, step, far)
        elif axis == "pair":
            p = partner(p, step, pair)
        else:
            m, q = divmod(partner(m * rep + q, step, mid * rep), rep)
        pairs.append((((f * mid + m) * pair + p) * rep + q, target))
    return pairs


def three_parts(value):
    first = value.astype(jnp.bfloat16).astype(jnp.float32)
    second = (value - first).astype(jnp.bfloat16).astype(jnp.float32)
    return first, second, value - first - second


def stack_rows(feat):
    return 6 * feat + 16


def norm_rows(values):
    width = next(value.shape[1] for value in values if not isinstance(value, float))
    halves = []
    for half in (values[:8], values[8:]):
        line = lax.broadcasted_iota(jnp.int32, (8, width), 0)
        rows = jnp.zeros((8, width), jnp.float32)
        for arrays in (False, True):
            for k, value in enumerate(half):
                if isinstance(value, float) != arrays:
                    rows = jnp.where(line == k, value, rows)
        halves.append(rows)
    return jnp.concatenate(halves, axis=0)


def norm_parts(z, first):
    high = jnp.sum(first * first, axis=0, keepdims=True)
    low = jnp.sum((z - first) * (z + first), axis=0, keepdims=True)
    one = high.astype(jnp.bfloat16).astype(jnp.float32)
    left = (high - one) + low
    two = left.astype(jnp.bfloat16).astype(jnp.float32)
    return one, two, left - two


def column_stack(z):
    a, b, c = three_parts(z)
    norms = norm_rows([*norm_parts(z, a), 1.0, 1.0, 1.0, 3.0, 3.0, 3.0, 1.0])
    return jnp.concatenate([a, norms, a, b, a, c, b], axis=0)


def row_stack(z, tripled):
    norms = norm_parts(z, three_parts(z)[0])
    a, b, c = three_parts(z * (-6.0 if tripled else -2.0))
    if tripled:
        norms = norm_rows([3.0] * 3 + [0.0] * 3 + [*norms])
    else:
        norms = norm_rows([1.0] * 3 + [*norms] + [0.0] * 3 + [1.0])
    return jnp.concatenate([a, norms, b, a, c, a, b], axis=0)


def packed_pieces(count, width):
    rest = width % LANES
    return LANES // rest if width > LANES and rest and LANES % rest == 0 and count % 8 == 0 else 0


def packed_shape(count, width):
    fit = packed_pieces(count, width)
    if not fit:
        return count, width
    return width // LANES * count + -(-(count // 8) // fit) * 8, LANES


def pack_kernel(block_ref, out_ref):
    block = block_ref[...]
    count, width = block.shape
    fit = packed_pieces(count, width)
    if not fit:
        out_ref[...] = block
        return
    full = width // LANES
    for k in range(full):
        out_ref[k * count : (k + 1) * count, :] = block[:, k * LANES : (k + 1) * LANES]
    base = full * count
    pieces = [block[at : at + 8, full * LANES :] for at in range(0, count, 8)]
    for first in range(0, len(pieces), fit):
        line = pieces[first : first + fit]
        line += [jnp.zeros_like(line[0])] * (fit - len(line))
        out_ref[base + first // fit * 8 : base + first // fit * 8 + 8, :] = jnp.concatenate(line, axis=1)


def line_shape(count, width, blocks):
    return -(-blocks * width // LANES) * count, LANES


def line_kernel(count, width, *refs):
    block_refs, out_ref = refs[:-1], refs[-1]
    fit = packed_pieces(count, width)
    full, rest = width // LANES, width % LANES
    if not fit:
        joined = [ref[...] for ref in block_refs]
    else:
        joined, at = [], 0
        for ref in block_refs:
            for k in range(full):
                out_ref[at : at + count, :] = ref[k * count : (k + 1) * count, :]
                at += count
            pieces = []
            for k in range(count // 8):
                begin = full * count + k // fit * 8
                pieces.append(ref[begin : begin + 8, k % fit * rest : (k % fit + 1) * rest])
            joined.append(jnp.concatenate(pieces, axis=0))
    begin = 0 if not fit else len(block_refs) * full * count
    over = -sum(item.shape[1] for item in joined) % LANES
    if over:
        joined.append(jnp.zeros((count, over), jnp.float32))
    tails = jnp.concatenate(joined, axis=1)
    for k in range(tails.shape[1] // LANES):
        out_ref[begin + k * count : begin + (k + 1) * count, :] = tails[:, k * LANES : (k + 1) * LANES]


def piece_values(scale, row_feat, piece):
    feat = scale.shape[0]
    rows = row_feat.shape[0] // 2
    col_feat = column_stack(piece[:feat] * scale).astype(jnp.bfloat16)
    vec = piece[feat:]
    vec_high = vec.astype(jnp.bfloat16)
    vec_low = (vec - vec_high.astype(jnp.float32)).astype(jnp.bfloat16)
    vec_parts = jnp.concatenate([vec_high, vec_low], axis=0)
    both = jnp.dot(row_feat, col_feat, preferred_element_type=jnp.float32)
    square = jnp.maximum(both[:rows], 1e-30)
    root = square * lax.rsqrt(square)
    value = (jnp.maximum(both[rows:], 1.0) + root) * jnp.exp2(root * (-1.0 / math.log(2.0)))
    high = value.astype(jnp.bfloat16)
    low = (value - high.astype(jnp.float32)).astype(jnp.bfloat16)
    return [high, low], [vec_parts, vec_parts]


def add_columns(total, scale, row_feat, line_refs, count):
    def products(pieces):
        values, vectors = [], []
        for piece in pieces:
            value, vector = piece_values(scale, row_feat, piece)
            values += value
            vectors += vector
        values, vectors = jnp.concatenate(values, axis=1), jnp.concatenate(vectors, axis=1)
        return lax.dot_general(vectors, values, (((1,), (1,)), ((), ())), preferred_element_type=jnp.float32)

    numbers = [ref.shape[0] // count for ref in line_refs]
    if sum(numbers) <= 16:
        pieces = [ref[k * count : (k + 1) * count, :] for ref, number in zip(line_refs, numbers) for k in range(number)]
        for piece in pieces:
            total = total + products([piece])
        return total
    for ref, number in zip(line_refs, numbers):

        def add(k, total, ref=ref):
            return total + products([ref[pl.ds(pl.multiple_of(k * count, 8), count), :]])

        total = lax.fori_loop(0, number, add, total)
    return total


def first_kernel(nrow, count, scale_ref, *refs):
    row_refs, line_refs = refs[:nrow], refs[nrow : -2 - nrow]
    total_refs, feat_ref, scale_out = refs[-2 - nrow : -2], refs[-2], refs[-1]
    feat, width = row_refs[0].shape
    scale = jnp.broadcast_to(jnp.sqrt(jnp.float32(5.0 / 3.0)) / scale_ref[...], (feat, LANES))
    scale_out[...] = scale
    for k, ref in enumerate(row_refs):
        z = ref[...] * scale[:, :1]
        begin = 2 * k * width
        feat_ref[begin : begin + width, :] = row_stack(z, True).T.astype(jnp.bfloat16)
        feat_ref[begin + width : begin + 2 * width, :] = row_stack(z, False).T.astype(jnp.bfloat16)
    for k, ref in enumerate(total_refs):
        rows = feat_ref[2 * k * width : 2 * (k + 1) * width, :]
        ref[...] = add_columns(jnp.zeros(ref.shape, jnp.float32), scale, rows, line_refs, count)


def middle_kernel(numbers, count, scale_ref, feat_ref, *refs):
    many = len(numbers)
    before_refs, line_refs, total_refs = refs[:many], refs[many:-many], refs[-many:]
    width = total_refs[0].shape[1]
    for k, before, after in zip(numbers, before_refs, total_refs):
        rows = feat_ref[2 * k * width : 2 * (k + 1) * width, :]
        after[...] = add_columns(before[...], scale_ref[...], rows, line_refs, count)


def last_kernel(count, number, scale_ref, feat_ref, before_ref, *refs):
    nvec, width = refs[-1].shape
    rows = feat_ref[2 * number * width : 2 * (number + 1) * width, :]
    part = add_columns(before_ref[...], scale_ref[...], rows, refs[:-1], count)
    refs[-1][...] = part[:nvec] + part[nvec:]


def limits(rows, cols):
    return {
        "compiler_params": pltpu.CompilerParams(vmem_limit_bytes=4 * MIB + 4096 * rows + 2048 * cols),
        "cost_estimate": pl.CostEstimate(flops=0, bytes_accessed=0, transcendentals=0),
    }


def per_device(sizes, points, vectors, lengthscales):
    far, mid, pair, rep = sizes
    (feat, width), nvec = points.shape, vectors.shape[0]
    count, rows = feat + nvec, pair * width
    high, wide = packed_shape(count, width)

    def send(item, axis, step):
        return lax.ppermute(item, AXES, permutation(sizes, axis, step))

    def call(body, lines, out_shape, *operands):
        cols = sum(line.shape[0] for line in lines) // count * LANES
        return pl.pallas_call(
            body,
            out_shape=[jax.ShapeDtypeStruct(shape, dtype) for shape, dtype in out_shape],
            **limits(rows, cols),
        )(*operands, *lines)

    block = pl.pallas_call(
        pack_kernel,
        out_shape=jax.ShapeDtypeStruct((high, wide), jnp.float32),
        compiler_params=pltpu.CompilerParams(vmem_limit_bytes=2 * MIB),
    )(jnp.concatenate([points, vectors], axis=0))
    later_points, block = lax.optimization_barrier((points, block))
    blocks = [send(block, "far", k) for k in [*range(2, far), 1][: far - 1]]
    row_points = [send(later_points, "pair", k) for k in range(1, pair)]
    blocks, row_points = lax.optimization_barrier((blocks, row_points))
    line = pl.pallas_call(
        functools.partial(line_kernel, count, width),
        out_shape=jax.ShapeDtypeStruct(line_shape(count, width, far), jnp.float32),
        compiler_params=pltpu.CompilerParams(vmem_limit_bytes=2 * MIB + 16 * far * high * wide),
    )(block, *blocks)
    steps = list(range(1, mid * rep))
    plane = [send(line, "plane", k) for k in steps[1:] + steps[:1]]
    totals = [((2 * nvec, width), jnp.float32)] * pair
    *total, row_feat, scale = call(
        functools.partial(first_kernel, pair, count),
        [line],
        totals + [((2 * rows, stack_rows(feat)), jnp.bfloat16), ((feat, LANES), jnp.float32)],
        lengthscales[:, None],
        points,
        *row_points,
    )

    def middle(total, lines, first):
        numbers = list(range(first, pair))
        if not lines or not numbers:
            return total
        total, lines = lax.optimization_barrier((total, lines))
        body = functools.partial(middle_kernel, numbers, count)
        return [*total[:first], *call(body, lines, totals[first:], scale, row_feat, *total[first:])]

    total = middle(total, plane[:-2], 0)
    total = middle(total, plane[-2:-1], 1)
    total, plane[-1:] = lax.optimization_barrier((total, plane[-1:]))

    def finish(k, total):
        lines = plane[-1:] if k else plane[-2:]
        body = functools.partial(last_kernel, count, k)
        (part,) = call(body, lines, [((nvec, width), jnp.float32)], scale, row_feat, total[k])
        return part

    parts = []
    for k in range(1, pair):
        part = finish(k, total)
        total, part = lax.optimization_barrier((total, part))
        parts.append(part)
    result = finish(0, total)
    for k, part in enumerate(parts, 1):
        back = [(target, source) for source, target in permutation(sizes, "pair", k)]
        result = result + lax.ppermute(part, AXES, back)
    return result


def solution(mesh):
    sizes = split_blocks(mesh.shape["blk"], mesh.shape["rep"])
    return jax.shard_map(
        functools.partial(per_device, sizes),
        mesh=mesh,
        in_specs=(P(None, AXES), P(None, AXES), P()),
        out_specs=P(None, AXES),
        check_vma=False,
    )
```

profile of v0, /device:TPU:0, one launch (start us, length us, event | category | flops | bytes accessed | tf_op | source)
XLA Modules:
  0.0 21.1 jit_solution(7962855174581586164)
XLA Ops:
  0.0 0.8 %pad_maximum_fusion.block_ref = f32[48,160]{1,0:T(8,128)S(1)} fusion(f32[32,160]{1,0:T(8,128)} %param.4, f32[16,160]{1,0:T(8,128)} %refs_0_.1), kind=kLoop, calls=%fused_computation | loop fusion | flops 7680 | bytes 61440 | tf_op jit(solution)/shard_map/concatenate | solution.py:255
  0.8 0.0 copy-start
  0.8 0.1 shard_map.37.refs_0_
  0.8 4.0 %collective-permute-start = (f32[64,128]{1,0:T(8,128)S(1)}, f32[64,128]{1,0:T(8,128)S(1)}, u32[]{:S(2)}, u32[]{:S(2)}) collective-permute-start(f32[64,128]{1,0:T(8,128)S(1)} %shard_map.37.refs_0_), channel_id=1, source_target_pairs={{16,0},{17,1},{18,2},{19,3},{20,4},{21,5},{22,6},{23,7},{24,8},{25... | collective-permute-start | bytes 98312 | tf_op jit(solution)/shard_map/ppermute | solution.py:241
  4.9 1.3 %collective-permute-start.1 = (f32[64,128]{1,0:T(8,128)S(1)}, f32[64,128]{1,0:T(8,128)S(1)}, u32[]{:S(2)}, u32[]{:S(2)}) collective-permute-start(f32[64,128]{1,0:T(8,128)S(1)} %shard_map.37.refs_0_), channel_id=1, source_target_pairs={{24,0},{25,1},{26,2},{27,3},{28,4},{29,5},{30,6},{31,7},{16,8},{17... | collective-permute-start | bytes 98312 | tf_op jit(solution)/shard_map/ppermute | solution.py:241
  6.2 0.2 %collective-permute-start.2 = (f32[64,128]{1,0:T(8,128)S(1)}, f32[64,128]{1,0:T(8,128)S(1)}, u32[]{:S(2)}, u32[]{:S(2)}) collective-permute-start(f32[64,128]{1,0:T(8,128)S(1)} %shard_map.37.refs_0_), channel_id=1, source_target_pairs={{8,0},{9,1},{10,2},{11,3},{12,4},{13,5},{14,6},{15,7},{0,8},{1,9},... | collective-permute-start | bytes 98312 | tf_op jit(solution)/shard_map/ppermute | solution.py:241
  6.5 0.0 copy-done
  6.5 0.0 collective-permute-start.3
  6.5 1.2 %collective-permute-done.3.refs_1_ = f32[16,160]{1,0:T(8,128)S(1)} collective-permute-done((f32[16,160]{1,0:T(8,128)S(1)}, f32[16,160]{1,0:T(8,128)S(1)}, u32[]{:S(2)}, u32[]{:S(2)}) %collective-permute-start.3) | collective-permute-done | bytes 10272 | tf_op jit(solution)/shard_map/ppermute | solution.py:241
  7.7 0.0 collective-permute-done.refs_1_
  7.7 2.9 %collective-permute-done.1.refs_2_ = f32[64,128]{1,0:T(8,128)S(1)} collective-permute-done((f32[64,128]{1,0:T(8,128)S(1)}, f32[64,128]{1,0:T(8,128)S(1)}, u32[]{:S(2)}, u32[]{:S(2)}) %collective-permute-start.1) | collective-permute-done | bytes 32800 | tf_op jit(solution)/shard_map/ppermute | solution.py:241
  10.6 0.0 collective-permute-done.2.refs_3_
  10.6 0.1 shard_map.38.refs_2_
  10.8 0.0 copy-start.1
  10.8 1.6 %collective-permute-start.4 = (f32[240,128]{1,0:T(8,128)S(1)}, f32[240,128]{1,0:T(8,128)S(1)}, u32[]{:S(2)}, u32[]{:S(2)}) collective-permute-start(f32[240,128]{1,0:T(8,128)S(1)} %shard_map.38.refs_2_), channel_id=1, source_target_pairs={{4,0},{5,1},{6,2},{7,3},{0,4},{1,5},{2,6},{3,7},{12,8},{13,9},{14,... | collective-permute-start | bytes 368648 | tf_op jit(solution)/shard_map/ppermute | solution.py:241
  12.4 1.4 %collective-permute-start.5 = (f32[240,128]{1,0:T(8,128)S(1)}, f32[240,128]{1,0:T(8,128)S(1)}, u32[]{:S(2)}, u32[]{:S(2)}) collective-permute-start(f32[240,128]{1,0:T(8,128)S(1)} %shard_map.38.refs_2_), channel_id=1, source_target_pairs={{5,0},{4,1},{7,2},{6,3},{1,4},{0,5},{3,6},{2,7},{13,8},{12,9},{15,... | collective-permute-start | bytes 368648 | tf_op jit(solution)/shard_map/ppermute | solution.py:241
  13.8 0.5 %collective-permute-start.6 = (f32[240,128]{1,0:T(8,128)S(1)}, f32[240,128]{1,0:T(8,128)S(1)}, u32[]{:S(2)}, u32[]{:S(2)}) collective-permute-start(f32[240,128]{1,0:T(8,128)S(1)} %shard_map.38.refs_2_), channel_id=1, source_target_pairs={{1,0},{0,1},{3,2},{2,3},{5,4},{4,5},{7,6},{6,7},{9,8},{8,9},{11,10... | collective-permute-start | bytes 368648 | tf_op jit(solution)/shard_map/ppermute | solution.py:241
  14.3 0.0 copy-done.1
  14.3 0.1 copy.4.scale_ref
  14.4 1.1 %shard_map.39 = (f32[64,160]{1,0:T(8,128)S(1)}, f32[64,160]{1,0:T(8,128)S(1)}, bf16[640,112]{1,0:T(8,128)(2,1)S(1)}, f32[16,128]{1,0:T(8,128)S(1)}) custom-call(f32[16,1]{1,0:T(8,128)S(1)} %copy.4.scale_ref, f32[16,160]{1,0:T(8,128)S(1)} %copy-done, f32[16,160]{1,0:T(8,128)S(1)} %collective-permute-done.3.refs_1_, f32[240,128]{1,0:T(8,128)S(1)} %shard_map.38.refs_2_), custom_call_target="tpu_custom_call" | custom-call | tf_op jit(solution)/shard_map/pallas_call | solution.py:245
  15.5 1.1 %collective-permute-done.4.refs_2_ = f32[240,128]{1,0:T(8,128)S(1)} collective-permute-done((f32[240,128]{1,0:T(8,128)S(1)}, f32[240,128]{1,0:T(8,128)S(1)}, u32[]{:S(2)}, u32[]{:S(2)}) %collective-permute-start.4) | collective-permute-done | bytes 122912 | tf_op jit(solution)/shard_map/ppermute | solution.py:241
  16.6 0.8 %shard_map.40 = (f32[64,160]{1,0:T(8,128)S(1)}, f32[64,160]{1,0:T(8,128)S(1)}) custom-call(f32[16,128]{1,0:T(8,128)S(1)} %get-tuple-element.34.scale_ref, bf16[640,112]{1,0:T(8,128)(2,1)S(1)} %get-tuple-element.35.feat_ref, f32[64,160]{1,0:T(8,128)S(1)} %get-tuple-element.38.refs_0_, f32[64,160]{1,0:T(8,128)S(1)} %get-tuple-element.39.refs_1_, ...), custom_call_target="tpu_custom_call" | custom-call | tf_op jit(solution)/shard_map/pallas_call | solution.py:245
  17.4 0.8 %collective-permute-done.5.refs_1_.refs_0_ = f32[240,128]{1,0:T(8,128)S(1)} collective-permute-done((f32[240,128]{1,0:T(8,128)S(1)}, f32[240,128]{1,0:T(8,128)S(1)}, u32[]{:S(2)}, u32[]{:S(2)}) %collective-permute-start.5) | collective-permute-done | bytes 122912 | tf_op jit(solution)/shard_map/ppermute | solution.py:241
  18.1 0.5 %shard_map.41.before_ref = f32[64,160]{1,0:T(8,128)S(1)} custom-call(f32[16,128]{1,0:T(8,128)S(1)} %get-tuple-element.34.scale_ref, bf16[640,112]{1,0:T(8,128)(2,1)S(1)} %get-tuple-element.35.feat_ref, f32[64,160]{1,0:T(8,128)S(1)} %get-tuple-element.44.refs_0_, f32[240,128]{1,0:T(8,128)S(1)} %collective-permute-done.5.refs_1_.refs_0_), custom_call_target="tpu_custom_call" | custom-call | tf_op jit(solution)/shard_map/pallas_call | solution.py:245
  18.7 0.0 collective-permute-done.6.refs_0_.refs_1_
  18.7 0.5 %shard_map.42 = f32[32,160]{1,0:T(8,128)S(1)} custom-call(f32[16,128]{1,0:T(8,128)S(1)} %get-tuple-element.34.scale_ref, bf16[640,112]{1,0:T(8,128)(2,1)S(1)} %get-tuple-element.35.feat_ref, f32[64,160]{1,0:T(8,128)S(1)} %shard_map.41.before_ref, f32[240,128]{1,0:T(8,128)S(1)} %collective-permute-done.6.refs_0_.refs_1_), custom_call_target="tpu_custom_call" | custom-call | tf_op jit(solution)/shard_map/pallas_call | solution.py:245
  19.2 0.0 collective-permute-start.7
  19.2 0.7 %shard_map.43 = f32[32,160]{1,0:T(8,128)S(1)} custom-call(f32[16,128]{1,0:T(8,128)S(1)} %get-tuple-element.34.scale_ref, bf16[640,112]{1,0:T(8,128)(2,1)S(1)} %get-tuple-element.35.feat_ref, f32[64,160]{1,0:T(8,128)S(1)} %get-tuple-element.49.before_ref, f32[240,128]{1,0:T(8,128)S(1)} %collective-permute-done.5.refs_1_.refs_0_, ...), custom_call_target="tpu_custom_call" | custom-call | tf_op jit(solution)/shard_map/pallas_call | solution.py:245
  20.0 0.5 %collective-permute-done.7 = f32[32,160]{1,0:T(8,128)S(1)} collective-permute-done((f32[32,160]{1,0:T(8,128)S(1)}, f32[32,160]{1,0:T(8,128)S(1)}, u32[]{:S(2)}, u32[]{:S(2)}) %collective-permute-start.7) | collective-permute-done | bytes 20512 | tf_op jit(solution)/shard_map/ppermute | solution.py:303
  20.4 0.6 %add.3 = f32[32,160]{1,0:T(8,128)} add(f32[32,160]{1,0:T(8,128)S(1)} %shard_map.43, f32[32,160]{1,0:T(8,128)S(1)} %collective-permute-done.7) | non-fusion elementwise | flops 5120 | bytes 61440 | tf_op jit(solution)/shard_map/add | solution.py:303
Async XLA Ops:
  0.8 5.7 %copy-start = (f32[16,160]{1,0:T(8,128)S(1)}, f32[16,160]{1,0:T(8,128)}, u32[]{:S(2)}) copy-start(f32[16,160]{1,0:T(8,128)} %refs_0_.1) | copy-start | bytes 30724
  0.8 6.8 %collective-permute-start = (f32[64,128]{1,0:T(8,128)S(1)}, f32[64,128]{1,0:T(8,128)S(1)}, u32[]{:S(2)}, u32[]{:S(2)}) collective-permute-start(f32[64,128]{1,0:T(8,128)S(1)} %shard_map.37.refs_0_), channel_id=1, source_target_pairs={{16,0},{17,1},{18,2},{19,3},{20,4},{21,5},{22,6},{23,7},{24,8},{25... | collective-permute-start | bytes 98312 | tf_op jit(solution)/shard_map/ppermute | solution.py:241
  4.9 5.7 %collective-permute-start.1 = (f32[64,128]{1,0:T(8,128)S(1)}, f32[64,128]{1,0:T(8,128)S(1)}, u32[]{:S(2)}, u32[]{:S(2)}) collective-permute-start(f32[64,128]{1,0:T(8,128)S(1)} %shard_map.37.refs_0_), channel_id=1, source_target_pairs={{24,0},{25,1},{26,2},{27,3},{28,4},{29,5},{30,6},{31,7},{16,8},{17... | collective-permute-start | bytes 98312 | tf_op jit(solution)/shard_map/ppermute | solution.py:241
  6.2 4.4 %collective-permute-start.2 = (f32[64,128]{1,0:T(8,128)S(1)}, f32[64,128]{1,0:T(8,128)S(1)}, u32[]{:S(2)}, u32[]{:S(2)}) collective-permute-start(f32[64,128]{1,0:T(8,128)S(1)} %shard_map.37.refs_0_), channel_id=1, source_target_pairs={{8,0},{9,1},{10,2},{11,3},{12,4},{13,5},{14,6},{15,7},{0,8},{1,9},... | collective-permute-start | bytes 98312 | tf_op jit(solution)/shard_map/ppermute | solution.py:241
  6.5 1.2 %collective-permute-start.3 = (f32[16,160]{1,0:T(8,128)S(1)}, f32[16,160]{1,0:T(8,128)S(1)}, u32[]{:S(2)}, u32[]{:S(2)}) collective-permute-start(f32[16,160]{1,0:T(8,128)S(1)} %copy-done), channel_id=1, source_target_pairs={{2,0},{3,1},{0,2},{1,3},{6,4},{7,5},{4,6},{5,7},{10,8},{11,9},{8,1... | collective-permute-start | bytes 30728 | tf_op jit(solution)/shard_map/ppermute | solution.py:241
  10.8 3.6 %copy-start.1 = (f32[16]{0:T(128)S(1)}, f32[16]{0:T(128)}, u32[]{:S(2)}) copy-start(f32[16]{0:T(128)} %param.5) | copy-start | bytes 196
  10.8 5.8 %collective-permute-start.4 = (f32[240,128]{1,0:T(8,128)S(1)}, f32[240,128]{1,0:T(8,128)S(1)}, u32[]{:S(2)}, u32[]{:S(2)}) collective-permute-start(f32[240,128]{1,0:T(8,128)S(1)} %shard_map.38.refs_2_), channel_id=1, source_target_pairs={{4,0},{5,1},{6,2},{7,3},{0,4},{1,5},{2,6},{3,7},{12,8},{13,9},{14,... | collective-permute-start | bytes 368648 | tf_op jit(solution)/shard_map/ppermute | solution.py:241
  12.4 5.8 %collective-permute-start.5 = (f32[240,128]{1,0:T(8,128)S(1)}, f32[240,128]{1,0:T(8,128)S(1)}, u32[]{:S(2)}, u32[]{:S(2)}) collective-permute-start(f32[240,128]{1,0:T(8,128)S(1)} %shard_map.38.refs_2_), channel_id=1, source_target_pairs={{5,0},{4,1},{7,2},{6,3},{1,4},{0,5},{3,6},{2,7},{13,8},{12,9},{15,... | collective-permute-start | bytes 368648 | tf_op jit(solution)/shard_map/ppermute | solution.py:241
  13.8 4.9 %collective-permute-start.6 = (f32[240,128]{1,0:T(8,128)S(1)}, f32[240,128]{1,0:T(8,128)S(1)}, u32[]{:S(2)}, u32[]{:S(2)}) collective-permute-start(f32[240,128]{1,0:T(8,128)S(1)} %shard_map.38.refs_2_), channel_id=1, source_target_pairs={{1,0},{0,1},{3,2},{2,3},{5,4},{4,5},{7,6},{6,7},{9,8},{8,9},{11,10... | collective-permute-start | bytes 368648 | tf_op jit(solution)/shard_map/ppermute | solution.py:241
  19.2 1.2 %collective-permute-start.7 = (f32[32,160]{1,0:T(8,128)S(1)}, f32[32,160]{1,0:T(8,128)S(1)}, u32[]{:S(2)}, u32[]{:S(2)}) collective-permute-start(f32[32,160]{1,0:T(8,128)S(1)} %shard_map.42), channel_id=1, source_target_pairs={{0,2},{1,3},{2,0},{3,1},{4,6},{5,7},{6,4},{7,5},{8,10},{9,11},{10,... | collective-permute-start | bytes 61448 | tf_op jit(solution)/shard_map/ppermute | solution.py:303
where the time goes:
time: 21.3 us; the launch traced here: 21.1 us
  starting transfers between devices  9.21 us (43%)
  waiting for transfers between devices  6.43 us (30%)
  Pallas kernels  3.87 us (18%)
  other arithmetic  1.39 us (7%)
    ppermute x7, starting transfers between devices, send(): return lax.ppermute(item, AXES, permutation(sizes, axis, step))  9.18 us
    ppermute x7, waiting for transfers between devices, send(): return lax.ppermute(item, AXES, permutation(sizes, axis, step))  5.97 us
    pallas_call x5, Pallas kernels, call(): pl.pallas_call(body, out_shape=[jax.ShapeDtypeStruct(shape, dtype) for sh...  3.65 us
    concatenate x1, other arithmetic, per_device(): jnp.concatenate([points, vectors], axis=0)  0.77 us
    add x1, other arithmetic, per_device(): result = result + lax.ppermute(part, AXES, back)  0.62 us
    ppermute x1, waiting for transfers between devices, per_device(): result = result + lax.ppermute(part, AXES, back)  0.46 us
  transfers between devices with their start and end apart: 8, of which 5 were waited for; matrix products, arithmetic and copies ran while one was open for 0% of the time, Pallas kernels for 15%

commit v1 on v0

--- a/solution.py
+++ b/solution.py
@@ -222,6 +222,13 @@
     rows = feat_ref[2 * number * width : 2 * (number + 1) * width, :]
     part = add_columns(before_ref[...], scale_ref[...], rows, refs[:-1], count)
     refs[-1][...] = part[:nvec] + part[nvec:]
+
+
+def sum_kernel(*refs):
+    total = refs[0][...]
+    for ref in refs[1:-1]:
+        total = total + ref[...]
+    refs[-1][...] = total
 
 
 def limits(rows, cols):
@@ -298,10 +305,15 @@
         total, part = lax.optimization_barrier((total, part))
         parts.append(part)
     result = finish(0, total)
+    others = []
     for k, part in enumerate(parts, 1):
         back = [(target, source) for source, target in permutation(sizes, "pair", k)]
-        result = result + lax.ppermute(part, AXES, back)
-    return result
+        others.append(lax.ppermute(part, AXES, back))
+    return pl.pallas_call(
+        sum_kernel,
+        out_shape=jax.ShapeDtypeStruct((nvec, width), jnp.float32),
+        compiler_params=pltpu.CompilerParams(vmem_limit_bytes=2 * MIB),
+    )(result, *others)
 
 
 def solution(mesh):

time: 21.3 us -> 21.3 us (level)
  Pallas kernels: 3.87 us -> 4.49 us
  other arithmetic: 1.39 us -> 0.77 us
    pallas_call x0 -> x1, Pallas kernels: none -> 0.62 us  [per_device(): pl.pallas_call(sum_kernel, out_shape=jax.ShapeDtypeStruct((nvec, width),...]
    add x1 -> x0, other arithmetic: 0.62 us -> none  [per_device(): result = result + lax.ppermute(part, AXES, back)]
where the time goes in v1:
time: 21.3 us; the launch traced here: 21.1 us
  starting transfers between devices  9.21 us (43%)
  waiting for transfers between devices  6.43 us (30%)
  Pallas kernels  4.49 us (21%)
  other arithmetic  0.77 us (4%)
    ppermute x7, starting transfers between devices, send(): return lax.ppermute(item, AXES, permutation(sizes, axis, step))  9.18 us
    ppermute x7, waiting for transfers between devices, send(): return lax.ppermute(item, AXES, permutation(sizes, axis, step))  5.97 us
    pallas_call x5, Pallas kernels, call(): pl.pallas_call(body, out_shape=[jax.ShapeDtypeStruct(shape, dtype) for sh...  3.65 us
    concatenate x1, other arithmetic, per_device(): jnp.concatenate([points, vectors], axis=0)  0.77 us
    pallas_call x1, Pallas kernels, per_device(): pl.pallas_call(sum_kernel, out_shape=jax.ShapeDtypeStruct((nvec, width),...  0.62 us
    ppermute x1, waiting for transfers between devices, per_device(): others.append(lax.ppermute(part, AXES, back))  0.46 us
  transfers between devices with their start and end apart: 8, of which 5 were waited for; matrix products, arithmetic and copies ran while one was open for 0% of the time, Pallas kernels for 15%

profile of v1, /device:TPU:0, one launch (start us, length us, event | category | flops | bytes accessed | tf_op | source)
XLA Modules:
  0.0 21.1 jit_solution(12606561381829575615)
XLA Ops:
  0.0 0.8 %pad_maximum_fusion.block_ref = f32[48,160]{1,0:T(8,128)S(1)} fusion(f32[32,160]{1,0:T(8,128)} %param.4, f32[16,160]{1,0:T(8,128)} %refs_0_.1), kind=kLoop, calls=%fused_computation | loop fusion | flops 7680 | bytes 61440 | tf_op jit(solution)/shard_map/concatenate | solution.py:262
  0.8 0.0 copy-start
  0.8 0.1 shard_map.37.refs_0_
  0.8 4.0 %collective-permute-start = (f32[64,128]{1,0:T(8,128)S(1)}, f32[64,128]{1,0:T(8,128)S(1)}, u32[]{:S(2)}, u32[]{:S(2)}) collective-permute-start(f32[64,128]{1,0:T(8,128)S(1)} %shard_map.37.refs_0_), channel_id=1, source_target_pairs={{16,0},{17,1},{18,2},{19,3},{20,4},{21,5},{22,6},{23,7},{24,8},{25... | collective-permute-start | bytes 98312 | tf_op jit(solution)/shard_map/ppermute | solution.py:248
  4.9 1.3 %collective-permute-start.1 = (f32[64,128]{1,0:T(8,128)S(1)}, f32[64,128]{1,0:T(8,128)S(1)}, u32[]{:S(2)}, u32[]{:S(2)}) collective-permute-start(f32[64,128]{1,0:T(8,128)S(1)} %shard_map.37.refs_0_), channel_id=1, source_target_pairs={{24,0},{25,1},{26,2},{27,3},{28,4},{29,5},{30,6},{31,7},{16,8},{17... | collective-permute-start | bytes 98312 | tf_op jit(solution)/shard_map/ppermute | solution.py:248
  6.2 0.2 %collective-permute-start.2 = (f32[64,128]{1,0:T(8,128)S(1)}, f32[64,128]{1,0:T(8,128)S(1)}, u32[]{:S(2)}, u32[]{:S(2)}) collective-permute-start(f32[64,128]{1,0:T(8,128)S(1)} %shard_map.37.refs_0_), channel_id=1, source_target_pairs={{8,0},{9,1},{10,2},{11,3},{12,4},{13,5},{14,6},{15,7},{0,8},{1,9},... | collective-permute-start | bytes 98312 | tf_op jit(solution)/shard_map/ppermute | solution.py:248
  6.5 0.0 copy-done
  6.5 0.0 collective-permute-start.3
  6.5 1.2 %collective-permute-done.3.refs_1_ = f32[16,160]{1,0:T(8,128)S(1)} collective-permute-done((f32[16,160]{1,0:T(8,128)S(1)}, f32[16,160]{1,0:T(8,128)S(1)}, u32[]{:S(2)}, u32[]{:S(2)}) %collective-permute-start.3) | collective-permute-done | bytes 10272 | tf_op jit(solution)/shard_map/ppermute | solution.py:248
  7.7 0.0 collective-permute-done.refs_1_
  7.7 2.9 %collective-permute-done.1.refs_2_ = f32[64,128]{1,0:T(8,128)S(1)} collective-permute-done((f32[64,128]{1,0:T(8,128)S(1)}, f32[64,128]{1,0:T(8,128)S(1)}, u32[]{:S(2)}, u32[]{:S(2)}) %collective-permute-start.1) | collective-permute-done | bytes 32800 | tf_op jit(solution)/shard_map/ppermute | solution.py:248
  10.6 0.0 collective-permute-done.2.refs_3_
  10.6 0.1 shard_map.38.refs_2_
  10.8 0.0 copy-start.1
  10.8 1.6 %collective-permute-start.4 = (f32[240,128]{1,0:T(8,128)S(1)}, f32[240,128]{1,0:T(8,128)S(1)}, u32[]{:S(2)}, u32[]{:S(2)}) collective-permute-start(f32[240,128]{1,0:T(8,128)S(1)} %shard_map.38.refs_2_), channel_id=1, source_target_pairs={{4,0},{5,1},{6,2},{7,3},{0,4},{1,5},{2,6},{3,7},{12,8},{13,9},{14,... | collective-permute-start | bytes 368648 | tf_op jit(solution)/shard_map/ppermute | solution.py:248
  12.4 1.4 %collective-permute-start.5 = (f32[240,128]{1,0:T(8,128)S(1)}, f32[240,128]{1,0:T(8,128)S(1)}, u32[]{:S(2)}, u32[]{:S(2)}) collective-permute-start(f32[240,128]{1,0:T(8,128)S(1)} %shard_map.38.refs_2_), channel_id=1, source_target_pairs={{5,0},{4,1},{7,2},{6,3},{1,4},{0,5},{3,6},{2,7},{13,8},{12,9},{15,... | collective-permute-start | bytes 368648 | tf_op jit(solution)/shard_map/ppermute | solution.py:248
  13.8 0.5 %collective-permute-start.6 = (f32[240,128]{1,0:T(8,128)S(1)}, f32[240,128]{1,0:T(8,128)S(1)}, u32[]{:S(2)}, u32[]{:S(2)}) collective-permute-start(f32[240,128]{1,0:T(8,128)S(1)} %shard_map.38.refs_2_), channel_id=1, source_target_pairs={{1,0},{0,1},{3,2},{2,3},{5,4},{4,5},{7,6},{6,7},{9,8},{8,9},{11,10... | collective-permute-start | bytes 368648 | tf_op jit(solution)/shard_map/ppermute | solution.py:248
  14.3 0.0 copy-done.1
  14.3 0.1 copy.4.scale_ref
  14.4 1.1 %shard_map.39 = (f32[64,160]{1,0:T(8,128)S(1)}, f32[64,160]{1,0:T(8,128)S(1)}, bf16[640,112]{1,0:T(8,128)(2,1)S(1)}, f32[16,128]{1,0:T(8,128)S(1)}) custom-call(f32[16,1]{1,0:T(8,128)S(1)} %copy.4.scale_ref, f32[16,160]{1,0:T(8,128)S(1)} %copy-done, f32[16,160]{1,0:T(8,128)S(1)} %collective-permute-done.3.refs_1_, f32[240,128]{1,0:T(8,128)S(1)} %shard_map.38.refs_2_), custom_call_target="tpu_custom_call" | custom-call | tf_op jit(solution)/shard_map/pallas_call | solution.py:252
  15.5 1.1 %collective-permute-done.4.refs_2_ = f32[240,128]{1,0:T(8,128)S(1)} collective-permute-done((f32[240,128]{1,0:T(8,128)S(1)}, f32[240,128]{1,0:T(8,128)S(1)}, u32[]{:S(2)}, u32[]{:S(2)}) %collective-permute-start.4) | collective-permute-done | bytes 122912 | tf_op jit(solution)/shard_map/ppermute | solution.py:248
  16.6 0.8 %shard_map.40 = (f32[64,160]{1,0:T(8,128)S(1)}, f32[64,160]{1,0:T(8,128)S(1)}) custom-call(f32[16,128]{1,0:T(8,128)S(1)} %get-tuple-element.34.scale_ref, bf16[640,112]{1,0:T(8,128)(2,1)S(1)} %get-tuple-element.35.feat_ref, f32[64,160]{1,0:T(8,128)S(1)} %get-tuple-element.38.refs_0_, f32[64,160]{1,0:T(8,128)S(1)} %get-tuple-element.39.refs_1_, ...), custom_call_target="tpu_custom_call" | custom-call | tf_op jit(solution)/shard_map/pallas_call | solution.py:252
  17.4 0.8 %collective-permute-done.5.refs_1_.refs_0_ = f32[240,128]{1,0:T(8,128)S(1)} collective-permute-done((f32[240,128]{1,0:T(8,128)S(1)}, f32[240,128]{1,0:T(8,128)S(1)}, u32[]{:S(2)}, u32[]{:S(2)}) %collective-permute-start.5) | collective-permute-done | bytes 122912 | tf_op jit(solution)/shard_map/ppermute | solution.py:248
  18.1 0.5 %shard_map.41.before_ref = f32[64,160]{1,0:T(8,128)S(1)} custom-call(f32[16,128]{1,0:T(8,128)S(1)} %get-tuple-element.34.scale_ref, bf16[640,112]{1,0:T(8,128)(2,1)S(1)} %get-tuple-element.35.feat_ref, f32[64,160]{1,0:T(8,128)S(1)} %get-tuple-element.44.refs_0_, f32[240,128]{1,0:T(8,128)S(1)} %collective-permute-done.5.refs_1_.refs_0_), custom_call_target="tpu_custom_call" | custom-call | tf_op jit(solution)/shard_map/pallas_call | solution.py:252
  18.7 0.0 collective-permute-done.6.refs_0_.refs_1_
  18.7 0.5 %shard_map.42 = f32[32,160]{1,0:T(8,128)S(1)} custom-call(f32[16,128]{1,0:T(8,128)S(1)} %get-tuple-element.34.scale_ref, bf16[640,112]{1,0:T(8,128)(2,1)S(1)} %get-tuple-element.35.feat_ref, f32[64,160]{1,0:T(8,128)S(1)} %shard_map.41.before_ref, f32[240,128]{1,0:T(8,128)S(1)} %collective-permute-done.6.refs_0_.refs_1_), custom_call_target="tpu_custom_call" | custom-call | tf_op jit(solution)/shard_map/pallas_call | solution.py:252
  19.2 0.0 collective-permute-start.7
  19.2 0.7 %shard_map.43.refs_0_ = f32[32,160]{1,0:T(8,128)S(1)} custom-call(f32[16,128]{1,0:T(8,128)S(1)} %get-tuple-element.34.scale_ref, bf16[640,112]{1,0:T(8,128)(2,1)S(1)} %get-tuple-element.35.feat_ref, f32[64,160]{1,0:T(8,128)S(1)} %get-tuple-element.49.before_ref, f32[240,128]{1,0:T(8,128)S(1)} %collective-permute-done.5.refs_1_.refs_0_, ...), custom_call_target="tpu_custom_call" | custom-call | tf_op jit(solution)/shard_map/pallas_call | solution.py:252
  20.0 0.5 %collective-permute-done.7.refs_1_ = f32[32,160]{1,0:T(8,128)S(1)} collective-permute-done((f32[32,160]{1,0:T(8,128)S(1)}, f32[32,160]{1,0:T(8,128)S(1)}, u32[]{:S(2)}, u32[]{:S(2)}) %collective-permute-start.7) | collective-permute-done | bytes 20512 | tf_op jit(solution)/shard_map/ppermute | solution.py:311
  20.4 0.6 %shard_map.44 = f32[32,160]{1,0:T(8,128)} custom-call(f32[32,160]{1,0:T(8,128)S(1)} %shard_map.43.refs_0_, f32[32,160]{1,0:T(8,128)S(1)} %collective-permute-done.7.refs_1_), custom_call_target="tpu_custom_call" | custom-call | tf_op jit(solution)/shard_map/pallas_call | solution.py:312
Async XLA Ops:
  0.8 5.7 %copy-start = (f32[16,160]{1,0:T(8,128)S(1)}, f32[16,160]{1,0:T(8,128)}, u32[]{:S(2)}) copy-start(f32[16,160]{1,0:T(8,128)} %refs_0_.1) | copy-start | bytes 30724
  0.8 6.8 %collective-permute-start = (f32[64,128]{1,0:T(8,128)S(1)}, f32[64,128]{1,0:T(8,128)S(1)}, u32[]{:S(2)}, u32[]{:S(2)}) collective-permute-start(f32[64,128]{1,0:T(8,128)S(1)} %shard_map.37.refs_0_), channel_id=1, source_target_pairs={{16,0},{17,1},{18,2},{19,3},{20,4},{21,5},{22,6},{23,7},{24,8},{25... | collective-permute-start | bytes 98312 | tf_op jit(solution)/shard_map/ppermute | solution.py:248
  4.9 5.7 %collective-permute-start.1 = (f32[64,128]{1,0:T(8,128)S(1)}, f32[64,128]{1,0:T(8,128)S(1)}, u32[]{:S(2)}, u32[]{:S(2)}) collective-permute-start(f32[64,128]{1,0:T(8,128)S(1)} %shard_map.37.refs_0_), channel_id=1, source_target_pairs={{24,0},{25,1},{26,2},{27,3},{28,4},{29,5},{30,6},{31,7},{16,8},{17... | collective-permute-start | bytes 98312 | tf_op jit(solution)/shard_map/ppermute | solution.py:248
  6.2 4.4 %collective-permute-start.2 = (f32[64,128]{1,0:T(8,128)S(1)}, f32[64,128]{1,0:T(8,128)S(1)}, u32[]{:S(2)}, u32[]{:S(2)}) collective-permute-start(f32[64,128]{1,0:T(8,128)S(1)} %shard_map.37.refs_0_), channel_id=1, source_target_pairs={{8,0},{9,1},{10,2},{11,3},{12,4},{13,5},{14,6},{15,7},{0,8},{1,9},... | collective-permute-start | bytes 98312 | tf_op jit(solution)/shard_map/ppermute | solution.py:248
  6.5 1.2 %collective-permute-start.3 = (f32[16,160]{1,0:T(8,128)S(1)}, f32[16,160]{1,0:T(8,128)S(1)}, u32[]{:S(2)}, u32[]{:S(2)}) collective-permute-start(f32[16,160]{1,0:T(8,128)S(1)} %copy-done), channel_id=1, source_target_pairs={{2,0},{3,1},{0,2},{1,3},{6,4},{7,5},{4,6},{5,7},{10,8},{11,9},{8,1... | collective-permute-start | bytes 30728 | tf_op jit(solution)/shard_map/ppermute | solution.py:248
  10.8 3.6 %copy-start.1 = (f32[16]{0:T(128)S(1)}, f32[16]{0:T(128)}, u32[]{:S(2)}) copy-start(f32[16]{0:T(128)} %param.5) | copy-start | bytes 196
  10.8 5.8 %collective-permute-start.4 = (f32[240,128]{1,0:T(8,128)S(1)}, f32[240,128]{1,0:T(8,128)S(1)}, u32[]{:S(2)}, u32[]{:S(2)}) collective-permute-start(f32[240,128]{1,0:T(8,128)S(1)} %shard_map.38.refs_2_), channel_id=1, source_target_pairs={{4,0},{5,1},{6,2},{7,3},{0,4},{1,5},{2,6},{3,7},{12,8},{13,9},{14,... | collective-permute-start | bytes 368648 | tf_op jit(solution)/shard_map/ppermute | solution.py:248
  12.4 5.8 %collective-permute-start.5 = (f32[240,128]{1,0:T(8,128)S(1)}, f32[240,128]{1,0:T(8,128)S(1)}, u32[]{:S(2)}, u32[]{:S(2)}) collective-permute-start(f32[240,128]{1,0:T(8,128)S(1)} %shard_map.38.refs_2_), channel_id=1, source_target_pairs={{5,0},{4,1},{7,2},{6,3},{1,4},{0,5},{3,6},{2,7},{13,8},{12,9},{15,... | collective-permute-start | bytes 368648 | tf_op jit(solution)/shard_map/ppermute | solution.py:248
  13.8 4.9 %collective-permute-start.6 = (f32[240,128]{1,0:T(8,128)S(1)}, f32[240,128]{1,0:T(8,128)S(1)}, u32[]{:S(2)}, u32[]{:S(2)}) collective-permute-start(f32[240,128]{1,0:T(8,128)S(1)} %shard_map.38.refs_2_), channel_id=1, source_target_pairs={{1,0},{0,1},{3,2},{2,3},{5,4},{4,5},{7,6},{6,7},{9,8},{8,9},{11,10... | collective-permute-start | bytes 368648 | tf_op jit(solution)/shard_map/ppermute | solution.py:248
  19.2 1.2 %collective-permute-start.7 = (f32[32,160]{1,0:T(8,128)S(1)}, f32[32,160]{1,0:T(8,128)S(1)}, u32[]{:S(2)}, u32[]{:S(2)}) collective-permute-start(f32[32,160]{1,0:T(8,128)S(1)} %shard_map.42), channel_id=1, source_target_pairs={{0,2},{1,3},{2,0},{3,1},{4,6},{5,7},{6,4},{7,5},{8,10},{9,11},{10,... | collective-permute-start | bytes 61448 | tf_op jit(solution)/shard_map/ppermute | solution.py:311

commit v2 on v0

--- a/solution.py
+++ b/solution.py
@@ -256,7 +256,7 @@
     later_points, block = lax.optimization_barrier((points, block))
     blocks = [send(block, "far", k) for k in [*range(2, far), 1][: far - 1]]
     row_points = [send(later_points, "pair", k) for k in range(1, pair)]
-    blocks, row_points = lax.optimization_barrier((blocks, row_points))
+    blocks = lax.optimization_barrier(blocks)
     line = pl.pallas_call(
         functools.partial(line_kernel, count, width),
         out_shape=jax.ShapeDtypeStruct(line_shape(count, width, far), jnp.float32),

time: 21.3 us -> 21.3 us (level)
  no operation moved by 1% of the time
where the time goes in v2:
time: 21.3 us; the launch traced here: 21.1 us
  starting transfers between devices  9.21 us (43%)
  waiting for transfers between devices  6.42 us (30%)
  Pallas kernels  3.87 us (18%)
  other arithmetic  1.39 us (7%)
    ppermute x7, starting transfers between devices, send(): return lax.ppermute(item, AXES, permutation(sizes, axis, step))  9.18 us
    ppermute x7, waiting for transfers between devices, send(): return lax.ppermute(item, AXES, permutation(sizes, axis, step))  5.96 us
    pallas_call x5, Pallas kernels, call(): pl.pallas_call(body, out_shape=[jax.ShapeDtypeStruct(shape, dtype) for sh...  3.65 us
    concatenate x1, other arithmetic, per_device(): jnp.concatenate([points, vectors], axis=0)  0.77 us
    add x1, other arithmetic, per_device(): result = result + lax.ppermute(part, AXES, back)  0.62 us
    ppermute x1, waiting for transfers between devices, per_device(): result = result + lax.ppermute(part, AXES, back)  0.46 us
  transfers between devices with their start and end apart: 8, of which 5 were waited for; matrix products, arithmetic and copies ran while one was open for 0% of the time, Pallas kernels for 15%

profile of v2, /device:TPU:0, one launch (start us, length us, event | category | flops | bytes accessed | tf_op | source)
XLA Modules:
  0.0 21.1 jit_solution(1897333110304970954)
XLA Ops:
  0.0 0.8 %pad_maximum_fusion.block_ref = f32[48,160]{1,0:T(8,128)S(1)} fusion(f32[32,160]{1,0:T(8,128)} %param.4, f32[16,160]{1,0:T(8,128)} %refs_0_.1), kind=kLoop, calls=%fused_computation | loop fusion | flops 7680 | bytes 61440 | tf_op jit(solution)/shard_map/concatenate | solution.py:255
  0.8 0.1 shard_map.37.refs_0_
  0.8 0.0 copy-start
  0.8 4.0 %collective-permute-start.1 = (f32[64,128]{1,0:T(8,128)S(1)}, f32[64,128]{1,0:T(8,128)S(1)}, u32[]{:S(2)}, u32[]{:S(2)}) collective-permute-start(f32[64,128]{1,0:T(8,128)S(1)} %shard_map.37.refs_0_), channel_id=1, source_target_pairs={{16,0},{17,1},{18,2},{19,3},{20,4},{21,5},{22,6},{23,7},{24,8},{25... | collective-permute-start | bytes 98312 | tf_op jit(solution)/shard_map/ppermute | solution.py:241
  4.9 1.3 %collective-permute-start.2 = (f32[64,128]{1,0:T(8,128)S(1)}, f32[64,128]{1,0:T(8,128)S(1)}, u32[]{:S(2)}, u32[]{:S(2)}) collective-permute-start(f32[64,128]{1,0:T(8,128)S(1)} %shard_map.37.refs_0_), channel_id=1, source_target_pairs={{24,0},{25,1},{26,2},{27,3},{28,4},{29,5},{30,6},{31,7},{16,8},{17... | collective-permute-start | bytes 98312 | tf_op jit(solution)/shard_map/ppermute | solution.py:241
  6.2 0.2 %collective-permute-start.3 = (f32[64,128]{1,0:T(8,128)S(1)}, f32[64,128]{1,0:T(8,128)S(1)}, u32[]{:S(2)}, u32[]{:S(2)}) collective-permute-start(f32[64,128]{1,0:T(8,128)S(1)} %shard_map.37.refs_0_), channel_id=1, source_target_pairs={{8,0},{9,1},{10,2},{11,3},{12,4},{13,5},{14,6},{15,7},{0,8},{1,9},... | collective-permute-start | bytes 98312 | tf_op jit(solution)/shard_map/ppermute | solution.py:241
  6.5 0.7 %collective-permute-done.1.refs_1_ = f32[64,128]{1,0:T(8,128)S(1)} collective-permute-done((f32[64,128]{1,0:T(8,128)S(1)}, f32[64,128]{1,0:T(8,128)S(1)}, u32[]{:S(2)}, u32[]{:S(2)}) %collective-permute-start.1) | collective-permute-done | bytes 32800 | tf_op jit(solution)/shard_map/ppermute | solution.py:241
  7.1 3.5 %collective-permute-done.2.refs_2_ = f32[64,128]{1,0:T(8,128)S(1)} collective-permute-done((f32[64,128]{1,0:T(8,128)S(1)}, f32[64,128]{1,0:T(8,128)S(1)}, u32[]{:S(2)}, u32[]{:S(2)}) %collective-permute-start.2) | collective-permute-done | bytes 32800 | tf_op jit(solution)/shard_map/ppermute | solution.py:241
  10.6 0.0 collective-permute-done.3.refs_3_
  10.6 0.1 shard_map.38.refs_2_
  10.8 0.0 copy-start.1
  10.8 1.6 %collective-permute-start.4 = (f32[240,128]{1,0:T(8,128)S(1)}, f32[240,128]{1,0:T(8,128)S(1)}, u32[]{:S(2)}, u32[]{:S(2)}) collective-permute-start(f32[240,128]{1,0:T(8,128)S(1)} %shard_map.38.refs_2_), channel_id=1, source_target_pairs={{4,0},{5,1},{6,2},{7,3},{0,4},{1,5},{2,6},{3,7},{12,8},{13,9},{14,... | collective-permute-start | bytes 368648 | tf_op jit(solution)/shard_map/ppermute | solution.py:241
  12.4 1.4 %collective-permute-start.5 = (f32[240,128]{1,0:T(8,128)S(1)}, f32[240,128]{1,0:T(8,128)S(1)}, u32[]{:S(2)}, u32[]{:S(2)}) collective-permute-start(f32[240,128]{1,0:T(8,128)S(1)} %shard_map.38.refs_2_), channel_id=1, source_target_pairs={{5,0},{4,1},{7,2},{6,3},{1,4},{0,5},{3,6},{2,7},{13,8},{12,9},{15,... | collective-permute-start | bytes 368648 | tf_op jit(solution)/shard_map/ppermute | solution.py:241
  13.8 0.5 %collective-permute-start.6 = (f32[240,128]{1,0:T(8,128)S(1)}, f32[240,128]{1,0:T(8,128)S(1)}, u32[]{:S(2)}, u32[]{:S(2)}) collective-permute-start(f32[240,128]{1,0:T(8,128)S(1)} %shard_map.38.refs_2_), channel_id=1, source_target_pairs={{1,0},{0,1},{3,2},{2,3},{5,4},{4,5},{7,6},{6,7},{9,8},{8,9},{11,10... | collective-permute-start | bytes 368648 | tf_op jit(solution)/shard_map/ppermute | solution.py:241
  14.3 0.0 copy-done
  14.3 0.0 collective-permute-start
  14.3 0.0 copy-done.1
  14.3 0.1 copy.4.scale_ref
  14.4 1.1 %collective-permute-done.refs_1_ = f32[16,160]{1,0:T(8,128)S(1)} collective-permute-done((f32[16,160]{1,0:T(8,128)S(1)}, f32[16,160]{1,0:T(8,128)S(1)}, u32[]{:S(2)}, u32[]{:S(2)}) %collective-permute-start) | collective-permute-done | bytes 10272 | tf_op jit(solution)/shard_map/ppermute | solution.py:241
  15.5 1.1 %shard_map.39 = (f32[64,160]{1,0:T(8,128)S(1)}, f32[64,160]{1,0:T(8,128)S(1)}, bf16[640,112]{1,0:T(8,128)(2,1)S(1)}, f32[16,128]{1,0:T(8,128)S(1)}) custom-call(f32[16,1]{1,0:T(8,128)S(1)} %copy.4.scale_ref, f32[16,160]{1,0:T(8,128)S(1)} %copy-done, f32[16,160]{1,0:T(8,128)S(1)} %collective-permute-done.refs_1_, f32[240,128]{1,0:T(8,128)S(1)} %shard_map.38.refs_2_), custom_call_target="tpu_custom_call" | custom-call | tf_op jit(solution)/shard_map/pallas_call | solution.py:245
  16.6 0.0 collective-permute-done.4.refs_2_
  16.6 0.8 %shard_map.40 = (f32[64,160]{1,0:T(8,128)S(1)}, f32[64,160]{1,0:T(8,128)S(1)}) custom-call(f32[16,128]{1,0:T(8,128)S(1)} %get-tuple-element.32.scale_ref, bf16[640,112]{1,0:T(8,128)(2,1)S(1)} %get-tuple-element.33.feat_ref, f32[64,160]{1,0:T(8,128)S(1)} %get-tuple-element.36.refs_0_, f32[64,160]{1,0:T(8,128)S(1)} %get-tuple-element.37.refs_1_, ...), custom_call_target="tpu_custom_call" | custom-call | tf_op jit(solution)/shard_map/pallas_call | solution.py:245
  17.4 0.7 %collective-permute-done.5.refs_1_.refs_0_ = f32[240,128]{1,0:T(8,128)S(1)} collective-permute-done((f32[240,128]{1,0:T(8,128)S(1)}, f32[240,128]{1,0:T(8,128)S(1)}, u32[]{:S(2)}, u32[]{:S(2)}) %collective-permute-start.5) | collective-permute-done | bytes 122912 | tf_op jit(solution)/shard_map/ppermute | solution.py:241
  18.1 0.5 %shard_map.41.before_ref = f32[64,160]{1,0:T(8,128)S(1)} custom-call(f32[16,128]{1,0:T(8,128)S(1)} %get-tuple-element.32.scale_ref, bf16[640,112]{1,0:T(8,128)(2,1)S(1)} %get-tuple-element.33.feat_ref, f32[64,160]{1,0:T(8,128)S(1)} %get-tuple-element.42.refs_0_, f32[240,128]{1,0:T(8,128)S(1)} %collective-permute-done.5.refs_1_.refs_0_), custom_call_target="tpu_custom_call" | custom-call | tf_op jit(solution)/shard_map/pallas_call | solution.py:245
  18.7 0.0 collective-permute-done.6.refs_0_.refs_1_
  18.7 0.5 %shard_map.42 = f32[32,160]{1,0:T(8,128)S(1)} custom-call(f32[16,128]{1,0:T(8,128)S(1)} %get-tuple-element.32.scale_ref, bf16[640,112]{1,0:T(8,128)(2,1)S(1)} %get-tuple-element.33.feat_ref, f32[64,160]{1,0:T(8,128)S(1)} %shard_map.41.before_ref, f32[240,128]{1,0:T(8,128)S(1)} %collective-permute-done.6.refs_0_.refs_1_), custom_call_target="tpu_custom_call" | custom-call | tf_op jit(solution)/shard_map/pallas_call | solution.py:245
  19.2 0.0 collective-permute-start.7
  19.2 0.7 %shard_map.43 = f32[32,160]{1,0:T(8,128)S(1)} custom-call(f32[16,128]{1,0:T(8,128)S(1)} %get-tuple-element.32.scale_ref, bf16[640,112]{1,0:T(8,128)(2,1)S(1)} %get-tuple-element.33.feat_ref, f32[64,160]{1,0:T(8,128)S(1)} %get-tuple-element.47.before_ref, f32[240,128]{1,0:T(8,128)S(1)} %collective-permute-done.5.refs_1_.refs_0_, ...), custom_call_target="tpu_custom_call" | custom-call | tf_op jit(solution)/shard_map/pallas_call | solution.py:245
  20.0 0.5 %collective-permute-done.7 = f32[32,160]{1,0:T(8,128)S(1)} collective-permute-done((f32[32,160]{1,0:T(8,128)S(1)}, f32[32,160]{1,0:T(8,128)S(1)}, u32[]{:S(2)}, u32[]{:S(2)}) %collective-permute-start.7) | collective-permute-done | bytes 20512 | tf_op jit(solution)/shard_map/ppermute | solution.py:303
  20.4 0.6 %add.3 = f32[32,160]{1,0:T(8,128)} add(f32[32,160]{1,0:T(8,128)S(1)} %shard_map.43, f32[32,160]{1,0:T(8,128)S(1)} %collective-permute-done.7) | non-fusion elementwise | flops 5120 | bytes 61440 | tf_op jit(solution)/shard_map/add | solution.py:303
Async XLA Ops:
  0.8 13.5 %copy-start = (f32[16,160]{1,0:T(8,128)S(1)}, f32[16,160]{1,0:T(8,128)}, u32[]{:S(2)}) copy-start(f32[16,160]{1,0:T(8,128)} %refs_0_.1) | copy-start | bytes 30724
  0.8 6.3 %collective-permute-start.1 = (f32[64,128]{1,0:T(8,128)S(1)}, f32[64,128]{1,0:T(8,128)S(1)}, u32[]{:S(2)}, u32[]{:S(2)}) collective-permute-start(f32[64,128]{1,0:T(8,128)S(1)} %shard_map.37.refs_0_), channel_id=1, source_target_pairs={{16,0},{17,1},{18,2},{19,3},{20,4},{21,5},{22,6},{23,7},{24,8},{25... | collective-permute-start | bytes 98312 | tf_op jit(solution)/shard_map/ppermute | solution.py:241
  4.9 5.7 %collective-permute-start.2 = (f32[64,128]{1,0:T(8,128)S(1)}, f32[64,128]{1,0:T(8,128)S(1)}, u32[]{:S(2)}, u32[]{:S(2)}) collective-permute-start(f32[64,128]{1,0:T(8,128)S(1)} %shard_map.37.refs_0_), channel_id=1, source_target_pairs={{24,0},{25,1},{26,2},{27,3},{28,4},{29,5},{30,6},{31,7},{16,8},{17... | collective-permute-start | bytes 98312 | tf_op jit(solution)/shard_map/ppermute | solution.py:241
  6.2 4.4 %collective-permute-start.3 = (f32[64,128]{1,0:T(8,128)S(1)}, f32[64,128]{1,0:T(8,128)S(1)}, u32[]{:S(2)}, u32[]{:S(2)}) collective-permute-start(f32[64,128]{1,0:T(8,128)S(1)} %shard_map.37.refs_0_), channel_id=1, source_target_pairs={{8,0},{9,1},{10,2},{11,3},{12,4},{13,5},{14,6},{15,7},{0,8},{1,9},... | collective-permute-start | bytes 98312 | tf_op jit(solution)/shard_map/ppermute | solution.py:241
  10.8 3.6 %copy-start.1 = (f32[16]{0:T(128)S(1)}, f32[16]{0:T(128)}, u32[]{:S(2)}) copy-start(f32[16]{0:T(128)} %param.5) | copy-start | bytes 196
  10.8 5.9 %collective-permute-start.4 = (f32[240,128]{1,0:T(8,128)S(1)}, f32[240,128]{1,0:T(8,128)S(1)}, u32[]{:S(2)}, u32[]{:S(2)}) collective-permute-start(f32[240,128]{1,0:T(8,128)S(1)} %shard_map.38.refs_2_), channel_id=1, source_target_pairs={{4,0},{5,1},{6,2},{7,3},{0,4},{1,5},{2,6},{3,7},{12,8},{13,9},{14,... | collective-permute-start | bytes 368648 | tf_op jit(solution)/shard_map/ppermute | solution.py:241
  12.4 5.8 %collective-permute-start.5 = (f32[240,128]{1,0:T(8,128)S(1)}, f32[240,128]{1,0:T(8,128)S(1)}, u32[]{:S(2)}, u32[]{:S(2)}) collective-permute-start(f32[240,128]{1,0:T(8,128)S(1)} %shard_map.38.refs_2_), channel_id=1, source_target_pairs={{5,0},{4,1},{7,2},{6,3},{1,4},{0,5},{3,6},{2,7},{13,8},{12,9},{15,... | collective-permute-start | bytes 368648 | tf_op jit(solution)/shard_map/ppermute | solution.py:241
  13.8 4.9 %collective-permute-start.6 = (f32[240,128]{1,0:T(8,128)S(1)}, f32[240,128]{1,0:T(8,128)S(1)}, u32[]{:S(2)}, u32[]{:S(2)}) collective-permute-start(f32[240,128]{1,0:T(8,128)S(1)} %shard_map.38.refs_2_), channel_id=1, source_target_pairs={{1,0},{0,1},{3,2},{2,3},{5,4},{4,5},{7,6},{6,7},{9,8},{8,9},{11,10... | collective-permute-start | bytes 368648 | tf_op jit(solution)/shard_map/ppermute | solution.py:241
  14.3 1.2 %collective-permute-start = (f32[16,160]{1,0:T(8,128)S(1)}, f32[16,160]{1,0:T(8,128)S(1)}, u32[]{:S(2)}, u32[]{:S(2)}) collective-permute-start(f32[16,160]{1,0:T(8,128)S(1)} %copy-done), channel_id=1, source_target_pairs={{2,0},{3,1},{0,2},{1,3},{6,4},{7,5},{4,6},{5,7},{10,8},{11,9},{8,1... | collective-permute-start | bytes 30728 | tf_op jit(solution)/shard_map/ppermute | solution.py:241
  19.2 1.2 %collective-permute-start.7 = (f32[32,160]{1,0:T(8,128)S(1)}, f32[32,160]{1,0:T(8,128)S(1)}, u32[]{:S(2)}, u32[]{:S(2)}) collective-permute-start(f32[32,160]{1,0:T(8,128)S(1)} %shard_map.42), channel_id=1, source_target_pairs={{0,2},{1,3},{2,0},{3,1},{4,6},{5,7},{6,4},{7,5},{8,10},{9,11},{10,... | collective-permute-start | bytes 61448 | tf_op jit(solution)/shard_map/ppermute | solution.py:303

commit v3 on v2

--- a/solution.py
+++ b/solution.py
@@ -283,11 +283,10 @@
         return [*total[:first], *call(body, lines, totals[first:], scale, row_feat, *total[first:])]
 
     total = middle(total, plane[:-2], 0)
-    total = middle(total, plane[-2:-1], 1)
-    total, plane[-1:] = lax.optimization_barrier((total, plane[-1:]))
+    total, plane[-2:] = lax.optimization_barrier((total, plane[-2:]))
 
     def finish(k, total):
-        lines = plane[-1:] if k else plane[-2:]
+        lines = plane[-2:]
         body = functools.partial(last_kernel, count, k)
         (part,) = call(body, lines, [((nvec, width), jnp.float32)], scale, row_feat, total[k])
         return part

time: 21.3 us -> 21.5 us (level)
  waiting for transfers between devices: 6.42 us -> 6.95 us
  Pallas kernels: 3.87 us -> 3.58 us
    ppermute x7, waiting for transfers between devices: 5.96 us -> 6.49 us  [send(): return lax.ppermute(item, AXES, permutation(sizes, axis, step))]
    pallas_call x5 -> x4, Pallas kernels: 3.65 us -> 3.36 us  [call(): pl.pallas_call(body, out_shape=[jax.ShapeDtypeStruct(shape, dtype) for sh...]
  transfers between devices with their start and end apart: 8 -> 8, of which waited for: 5 -> 6; matrix products, arithmetic and copies ran while one was open for 0% -> 0% of each run, Pallas kernels for 15% -> 12%
where the time goes in v3:
time: 21.5 us; the launch traced here: 21.3 us
  starting transfers between devices  9.21 us (43%)
  waiting for transfers between devices  6.95 us (32%)
  Pallas kernels  3.58 us (17%)
  other arithmetic  1.39 us (6%)
    ppermute x7, starting transfers between devices, send(): return lax.ppermute(item, AXES, permutation(sizes, axis, step))  9.18 us
    ppermute x7, waiting for transfers between devices, send(): return lax.ppermute(item, AXES, permutation(sizes, axis, step))  6.49 us
    pallas_call x4, Pallas kernels, call(): pl.pallas_call(body, out_shape=[jax.ShapeDtypeStruct(shape, dtype) for sh...  3.36 us
    concatenate x1, other arithmetic, per_device(): jnp.concatenate([points, vectors], axis=0)  0.77 us
    add x1, other arithmetic, per_device(): result = result + lax.ppermute(part, AXES, back)  0.62 us
    ppermute x1, waiting for transfers between devices, per_device(): result = result + lax.ppermute(part, AXES, back)  0.46 us
  transfers between devices with their start and end apart: 8, of which 6 were waited for; matrix products, arithmetic and copies ran while one was open for 0% of the time, Pallas kernels for 12%

profile of v3, /device:TPU:0, one launch (start us, length us, event | category | flops | bytes accessed | tf_op | source)
XLA Modules:
  0.0 21.3 jit_solution(4955793306042132983)
XLA Ops:
  0.0 0.8 %pad_maximum_fusion.block_ref = f32[48,160]{1,0:T(8,128)S(1)} fusion(f32[32,160]{1,0:T(8,128)} %param.4, f32[16,160]{1,0:T(8,128)} %refs_0_.1), kind=kLoop, calls=%fused_computation | loop fusion | flops 7680 | bytes 61440 | tf_op jit(solution)/shard_map/concatenate | solution.py:255
  0.8 0.1 shard_map.37.refs_0_
  0.8 0.0 copy-start
  0.8 4.0 %collective-permute-start.1 = (f32[64,128]{1,0:T(8,128)S(1)}, f32[64,128]{1,0:T(8,128)S(1)}, u32[]{:S(2)}, u32[]{:S(2)}) collective-permute-start(f32[64,128]{1,0:T(8,128)S(1)} %shard_map.37.refs_0_), channel_id=1, source_target_pairs={{16,0},{17,1},{18,2},{19,3},{20,4},{21,5},{22,6},{23,7},{24,8},{25... | collective-permute-start | bytes 98312 | tf_op jit(solution)/shard_map/ppermute | solution.py:241
  4.9 1.3 %collective-permute-start.2 = (f32[64,128]{1,0:T(8,128)S(1)}, f32[64,128]{1,0:T(8,128)S(1)}, u32[]{:S(2)}, u32[]{:S(2)}) collective-permute-start(f32[64,128]{1,0:T(8,128)S(1)} %shard_map.37.refs_0_), channel_id=1, source_target_pairs={{24,0},{25,1},{26,2},{27,3},{28,4},{29,5},{30,6},{31,7},{16,8},{17... | collective-permute-start | bytes 98312 | tf_op jit(solution)/shard_map/ppermute | solution.py:241
  6.2 0.2 %collective-permute-start.3 = (f32[64,128]{1,0:T(8,128)S(1)}, f32[64,128]{1,0:T(8,128)S(1)}, u32[]{:S(2)}, u32[]{:S(2)}) collective-permute-start(f32[64,128]{1,0:T(8,128)S(1)} %shard_map.37.refs_0_), channel_id=1, source_target_pairs={{8,0},{9,1},{10,2},{11,3},{12,4},{13,5},{14,6},{15,7},{0,8},{1,9},... | collective-permute-start | bytes 98312 | tf_op jit(solution)/shard_map/ppermute | solution.py:241
  6.5 0.7 %collective-permute-done.1.refs_1_ = f32[64,128]{1,0:T(8,128)S(1)} collective-permute-done((f32[64,128]{1,0:T(8,128)S(1)}, f32[64,128]{1,0:T(8,128)S(1)}, u32[]{:S(2)}, u32[]{:S(2)}) %collective-permute-start.1) | collective-permute-done | bytes 32800 | tf_op jit(solution)/shard_map/ppermute | solution.py:241
  7.1 3.5 %collective-permute-done.2.refs_2_ = f32[64,128]{1,0:T(8,128)S(1)} collective-permute-done((f32[64,128]{1,0:T(8,128)S(1)}, f32[64,128]{1,0:T(8,128)S(1)}, u32[]{:S(2)}, u32[]{:S(2)}) %collective-permute-start.2) | collective-permute-done | bytes 32800 | tf_op jit(solution)/shard_map/ppermute | solution.py:241
  10.6 0.0 collective-permute-done.3.refs_3_
  10.6 0.1 shard_map.38.refs_2_
  10.8 0.0 copy-start.1
  10.8 1.6 %collective-permute-start.4 = (f32[240,128]{1,0:T(8,128)S(1)}, f32[240,128]{1,0:T(8,128)S(1)}, u32[]{:S(2)}, u32[]{:S(2)}) collective-permute-start(f32[240,128]{1,0:T(8,128)S(1)} %shard_map.38.refs_2_), channel_id=1, source_target_pairs={{4,0},{5,1},{6,2},{7,3},{0,4},{1,5},{2,6},{3,7},{12,8},{13,9},{14,... | collective-permute-start | bytes 368648 | tf_op jit(solution)/shard_map/ppermute | solution.py:241
  12.4 1.4 %collective-permute-start.5 = (f32[240,128]{1,0:T(8,128)S(1)}, f32[240,128]{1,0:T(8,128)S(1)}, u32[]{:S(2)}, u32[]{:S(2)}) collective-permute-start(f32[240,128]{1,0:T(8,128)S(1)} %shard_map.38.refs_2_), channel_id=1, source_target_pairs={{5,0},{4,1},{7,2},{6,3},{1,4},{0,5},{3,6},{2,7},{13,8},{12,9},{15,... | collective-permute-start | bytes 368648 | tf_op jit(solution)/shard_map/ppermute | solution.py:241
  13.8 0.5 %collective-permute-start.6 = (f32[240,128]{1,0:T(8,128)S(1)}, f32[240,128]{1,0:T(8,128)S(1)}, u32[]{:S(2)}, u32[]{:S(2)}) collective-permute-start(f32[240,128]{1,0:T(8,128)S(1)} %shard_map.38.refs_2_), channel_id=1, source_target_pairs={{1,0},{0,1},{3,2},{2,3},{5,4},{4,5},{7,6},{6,7},{9,8},{8,9},{11,10... | collective-permute-start | bytes 368648 | tf_op jit(solution)/shard_map/ppermute | solution.py:241
  14.3 0.0 copy-done
  14.3 0.0 collective-permute-start
  14.3 0.0 copy-done.1
  14.3 0.1 copy.4.scale_ref
  14.4 1.1 %collective-permute-done.refs_1_ = f32[16,160]{1,0:T(8,128)S(1)} collective-permute-done((f32[16,160]{1,0:T(8,128)S(1)}, f32[16,160]{1,0:T(8,128)S(1)}, u32[]{:S(2)}, u32[]{:S(2)}) %collective-permute-start) | collective-permute-done | bytes 10272 | tf_op jit(solution)/shard_map/ppermute | solution.py:241
  15.5 1.1 %shard_map.39 = (f32[64,160]{1,0:T(8,128)S(1)}, f32[64,160]{1,0:T(8,128)S(1)}, bf16[640,112]{1,0:T(8,128)(2,1)S(1)}, f32[16,128]{1,0:T(8,128)S(1)}) custom-call(f32[16,1]{1,0:T(8,128)S(1)} %copy.4.scale_ref, f32[16,160]{1,0:T(8,128)S(1)} %copy-done, f32[16,160]{1,0:T(8,128)S(1)} %collective-permute-done.refs_1_, f32[240,128]{1,0:T(8,128)S(1)} %shard_map.38.refs_2_), custom_call_target="tpu_custom_call" | custom-call | tf_op jit(solution)/shard_map/pallas_call | solution.py:245
  16.6 0.0 collective-permute-done.4.refs_2_
  16.6 0.8 %shard_map.40 = (f32[64,160]{1,0:T(8,128)S(1)}, f32[64,160]{1,0:T(8,128)S(1)}) custom-call(f32[16,128]{1,0:T(8,128)S(1)} %get-tuple-element.30.scale_ref, bf16[640,112]{1,0:T(8,128)(2,1)S(1)} %get-tuple-element.31.feat_ref, f32[64,160]{1,0:T(8,128)S(1)} %get-tuple-element.34.refs_0_, f32[64,160]{1,0:T(8,128)S(1)} %get-tuple-element.35.refs_1_, ...), custom_call_target="tpu_custom_call" | custom-call | tf_op jit(solution)/shard_map/pallas_call | solution.py:245
  17.4 0.7 %collective-permute-done.5.refs_0_ = f32[240,128]{1,0:T(8,128)S(1)} collective-permute-done((f32[240,128]{1,0:T(8,128)S(1)}, f32[240,128]{1,0:T(8,128)S(1)}, u32[]{:S(2)}, u32[]{:S(2)}) %collective-permute-start.5) | collective-permute-done | bytes 122912 | tf_op jit(solution)/shard_map/ppermute | solution.py:241
  18.1 0.5 %collective-permute-done.6.refs_1_ = f32[240,128]{1,0:T(8,128)S(1)} collective-permute-done((f32[240,128]{1,0:T(8,128)S(1)}, f32[240,128]{1,0:T(8,128)S(1)}, u32[]{:S(2)}, u32[]{:S(2)}) %collective-permute-start.6) | collective-permute-done | bytes 122912 | tf_op jit(solution)/shard_map/ppermute | solution.py:241
  18.7 0.7 %shard_map.41 = f32[32,160]{1,0:T(8,128)S(1)} custom-call(f32[16,128]{1,0:T(8,128)S(1)} %get-tuple-element.30.scale_ref, bf16[640,112]{1,0:T(8,128)(2,1)S(1)} %get-tuple-element.31.feat_ref, f32[64,160]{1,0:T(8,128)S(1)} %get-tuple-element.40.before_ref, f32[240,128]{1,0:T(8,128)S(1)} %collective-permute-done.5.refs_0_, ...), custom_call_target="tpu_custom_call" | custom-call | tf_op jit(solution)/shard_map/pallas_call | solution.py:245
  19.4 0.0 collective-permute-start.7
  19.5 0.7 %shard_map.42 = f32[32,160]{1,0:T(8,128)S(1)} custom-call(f32[16,128]{1,0:T(8,128)S(1)} %get-tuple-element.30.scale_ref, bf16[640,112]{1,0:T(8,128)(2,1)S(1)} %get-tuple-element.31.feat_ref, f32[64,160]{1,0:T(8,128)S(1)} %get-tuple-element.43.before_ref, f32[240,128]{1,0:T(8,128)S(1)} %collective-permute-done.5.refs_0_, ...), custom_call_target="tpu_custom_call" | custom-call | tf_op jit(solution)/shard_map/pallas_call | solution.py:245
  20.2 0.5 %collective-permute-done.7 = f32[32,160]{1,0:T(8,128)S(1)} collective-permute-done((f32[32,160]{1,0:T(8,128)S(1)}, f32[32,160]{1,0:T(8,128)S(1)}, u32[]{:S(2)}, u32[]{:S(2)}) %collective-permute-start.7) | collective-permute-done | bytes 20512 | tf_op jit(solution)/shard_map/ppermute | solution.py:302
  20.7 0.6 %add.3 = f32[32,160]{1,0:T(8,128)} add(f32[32,160]{1,0:T(8,128)S(1)} %shard_map.42, f32[32,160]{1,0:T(8,128)S(1)} %collective-permute-done.7) | non-fusion elementwise | flops 5120 | bytes 61440 | tf_op jit(solution)/shard_map/add | solution.py:302
Async XLA Ops:
  0.8 13.5 %copy-start = (f32[16,160]{1,0:T(8,128)S(1)}, f32[16,160]{1,0:T(8,128)}, u32[]{:S(2)}) copy-start(f32[16,160]{1,0:T(8,128)} %refs_0_.1) | copy-start | bytes 30724
  0.8 6.3 %collective-permute-start.1 = (f32[64,128]{1,0:T(8,128)S(1)}, f32[64,128]{1,0:T(8,128)S(1)}, u32[]{:S(2)}, u32[]{:S(2)}) collective-permute-start(f32[64,128]{1,0:T(8,128)S(1)} %shard_map.37.refs_0_), channel_id=1, source_target_pairs={{16,0},{17,1},{18,2},{19,3},{20,4},{21,5},{22,6},{23,7},{24,8},{25... | collective-permute-start | bytes 98312 | tf_op jit(solution)/shard_map/ppermute | solution.py:241
  4.9 5.7 %collective-permute-start.2 = (f32[64,128]{1,0:T(8,128)S(1)}, f32[64,128]{1,0:T(8,128)S(1)}, u32[]{:S(2)}, u32[]{:S(2)}) collective-permute-start(f32[64,128]{1,0:T(8,128)S(1)} %shard_map.37.refs_0_), channel_id=1, source_target_pairs={{24,0},{25,1},{26,2},{27,3},{28,4},{29,5},{30,6},{31,7},{16,8},{17... | collective-permute-start | bytes 98312 | tf_op jit(solution)/shard_map/ppermute | solution.py:241
  6.2 4.4 %collective-permute-start.3 = (f32[64,128]{1,0:T(8,128)S(1)}, f32[64,128]{1,0:T(8,128)S(1)}, u32[]{:S(2)}, u32[]{:S(2)}) collective-permute-start(f32[64,128]{1,0:T(8,128)S(1)} %shard_map.37.refs_0_), channel_id=1, source_target_pairs={{8,0},{9,1},{10,2},{11,3},{12,4},{13,5},{14,6},{15,7},{0,8},{1,9},... | collective-permute-start | bytes 98312 | tf_op jit(solution)/shard_map/ppermute | solution.py:241
  10.8 3.6 %copy-start.1 = (f32[16]{0:T(128)S(1)}, f32[16]{0:T(128)}, u32[]{:S(2)}) copy-start(f32[16]{0:T(128)} %param.5) | copy-start | bytes 196
  10.8 5.9 %collective-permute-start.4 = (f32[240,128]{1,0:T(8,128)S(1)}, f32[240,128]{1,0:T(8,128)S(1)}, u32[]{:S(2)}, u32[]{:S(2)}) collective-permute-start(f32[240,128]{1,0:T(8,128)S(1)} %shard_map.38.refs_2_), channel_id=1, source_target_pairs={{4,0},{5,1},{6,2},{7,3},{0,4},{1,5},{2,6},{3,7},{12,8},{13,9},{14,... | collective-permute-start | bytes 368648 | tf_op jit(solution)/shard_map/ppermute | solution.py:241
  12.4 5.8 %collective-permute-start.5 = (f32[240,128]{1,0:T(8,128)S(1)}, f32[240,128]{1,0:T(8,128)S(1)}, u32[]{:S(2)}, u32[]{:S(2)}) collective-permute-start(f32[240,128]{1,0:T(8,128)S(1)} %shard_map.38.refs_2_), channel_id=1, source_target_pairs={{5,0},{4,1},{7,2},{6,3},{1,4},{0,5},{3,6},{2,7},{13,8},{12,9},{15,... | collective-permute-start | bytes 368648 | tf_op jit(solution)/shard_map/ppermute | solution.py:241
  13.8 4.9 %collective-permute-start.6 = (f32[240,128]{1,0:T(8,128)S(1)}, f32[240,128]{1,0:T(8,128)S(1)}, u32[]{:S(2)}, u32[]{:S(2)}) collective-permute-start(f32[240,128]{1,0:T(8,128)S(1)} %shard_map.38.refs_2_), channel_id=1, source_target_pairs={{1,0},{0,1},{3,2},{2,3},{5,4},{4,5},{7,6},{6,7},{9,8},{8,9},{11,10... | collective-permute-start | bytes 368648 | tf_op jit(solution)/shard_map/ppermute | solution.py:241
  14.3 1.2 %collective-permute-start = (f32[16,160]{1,0:T(8,128)S(1)}, f32[16,160]{1,0:T(8,128)S(1)}, u32[]{:S(2)}, u32[]{:S(2)}) collective-permute-start(f32[16,160]{1,0:T(8,128)S(1)} %copy-done), channel_id=1, source_target_pairs={{2,0},{3,1},{0,2},{1,3},{6,4},{7,5},{4,6},{5,7},{10,8},{11,9},{8,1... | collective-permute-start | bytes 30728 | tf_op jit(solution)/shard_map/ppermute | solution.py:241
  19.4 1.2 %collective-permute-start.7 = (f32[32,160]{1,0:T(8,128)S(1)}, f32[32,160]{1,0:T(8,128)S(1)}, u32[]{:S(2)}, u32[]{:S(2)}) collective-permute-start(f32[32,160]{1,0:T(8,128)S(1)} %shard_map.41), channel_id=1, source_target_pairs={{0,2},{1,3},{2,0},{3,1},{4,6},{5,7},{6,4},{7,5},{8,10},{9,11},{10,... | collective-permute-start | bytes 61448 | tf_op jit(solution)/shard_map/ppermute | solution.py:302

commit v4 on v2

--- a/solution.py
+++ b/solution.py
@@ -254,7 +254,7 @@
         compiler_params=pltpu.CompilerParams(vmem_limit_bytes=2 * MIB),
     )(jnp.concatenate([points, vectors], axis=0))
     later_points, block = lax.optimization_barrier((points, block))
-    blocks = [send(block, "far", k) for k in [*range(2, far), 1][: far - 1]]
+    blocks = [send(block, "far", k) for k in reversed(range(1, far))]
     row_points = [send(later_points, "pair", k) for k in range(1, pair)]
     blocks = lax.optimization_barrier(blocks)
     line = pl.pallas_call(

time: 21.3 us -> 21.4 us (level)
  no operation moved by 1% of the time
where the time goes in v4:
time: 21.4 us; the launch traced here: 21.2 us
  starting transfers between devices  9.29 us (43%)
  waiting for transfers between devices  6.46 us (30%)
  Pallas kernels  3.87 us (18%)
  other arithmetic  1.39 us (6%)
    ppermute x7, starting transfers between devices, send(): return lax.ppermute(item, AXES, permutation(sizes, axis, step))  9.26 us
    ppermute x7, waiting for transfers between devices, send(): return lax.ppermute(item, AXES, permutation(sizes, axis, step))  6 us
    pallas_call x5, Pallas kernels, call(): pl.pallas_call(body, out_shape=[jax.ShapeDtypeStruct(shape, dtype) for sh...  3.65 us
    concatenate x1, other arithmetic, per_device(): jnp.concatenate([points, vectors], axis=0)  0.77 us
    add x1, other arithmetic, per_device(): result = result + lax.ppermute(part, AXES, back)  0.62 us
    ppermute x1, waiting for transfers between devices, per_device(): result = result + lax.ppermute(part, AXES, back)  0.46 us
  transfers between devices with their start and end apart: 8, of which 5 were waited for; matrix products, arithmetic and copies ran while one was open for 0% of the time, Pallas kernels for 15%

profile of v4, /device:TPU:0, one launch (start us, length us, event | category | flops | bytes accessed | tf_op | source)
XLA Modules:
  0.0 21.2 jit_solution(1107294619547300012)
XLA Ops:
  0.0 0.8 %pad_maximum_fusion.block_ref = f32[48,160]{1,0:T(8,128)S(1)} fusion(f32[32,160]{1,0:T(8,128)} %param.4, f32[16,160]{1,0:T(8,128)} %refs_0_.1), kind=kLoop, calls=%fused_computation | loop fusion | flops 7680 | bytes 61440 | tf_op jit(solution)/shard_map/concatenate | solution.py:255
  0.8 0.1 shard_map.37.refs_0_
  0.8 0.0 copy-start
  0.8 5.1 %collective-permute-start.1 = (f32[64,128]{1,0:T(8,128)S(1)}, f32[64,128]{1,0:T(8,128)S(1)}, u32[]{:S(2)}, u32[]{:S(2)}) collective-permute-start(f32[64,128]{1,0:T(8,128)S(1)} %shard_map.37.refs_0_), channel_id=1, source_target_pairs={{24,0},{25,1},{26,2},{27,3},{28,4},{29,5},{30,6},{31,7},{16,8},{17... | collective-permute-start | bytes 98312 | tf_op jit(solution)/shard_map/ppermute | solution.py:241
  5.9 0.0 collective-permute-start.2
  5.9 0.6 %collective-permute-start.3 = (f32[64,128]{1,0:T(8,128)S(1)}, f32[64,128]{1,0:T(8,128)S(1)}, u32[]{:S(2)}, u32[]{:S(2)}) collective-permute-start(f32[64,128]{1,0:T(8,128)S(1)} %shard_map.37.refs_0_), channel_id=1, source_target_pairs={{8,0},{9,1},{10,2},{11,3},{12,4},{13,5},{14,6},{15,7},{0,8},{1,9},... | collective-permute-start | bytes 98312 | tf_op jit(solution)/shard_map/ppermute | solution.py:241
  6.5 1.3 %collective-permute-done.1.refs_1_ = f32[64,128]{1,0:T(8,128)S(1)} collective-permute-done((f32[64,128]{1,0:T(8,128)S(1)}, f32[64,128]{1,0:T(8,128)S(1)}, u32[]{:S(2)}, u32[]{:S(2)}) %collective-permute-start.1) | collective-permute-done | bytes 32800 | tf_op jit(solution)/shard_map/ppermute | solution.py:241
  7.8 2.9 %collective-permute-done.2.refs_2_ = f32[64,128]{1,0:T(8,128)S(1)} collective-permute-done((f32[64,128]{1,0:T(8,128)S(1)}, f32[64,128]{1,0:T(8,128)S(1)}, u32[]{:S(2)}, u32[]{:S(2)}) %collective-permute-start.2) | collective-permute-done | bytes 32800 | tf_op jit(solution)/shard_map/ppermute | solution.py:241
  10.7 0.0 collective-permute-done.3.refs_3_
  10.7 0.1 shard_map.38.refs_2_
  10.9 0.0 copy-start.1
  10.9 1.6 %collective-permute-start.4 = (f32[240,128]{1,0:T(8,128)S(1)}, f32[240,128]{1,0:T(8,128)S(1)}, u32[]{:S(2)}, u32[]{:S(2)}) collective-permute-start(f32[240,128]{1,0:T(8,128)S(1)} %shard_map.38.refs_2_), channel_id=1, source_target_pairs={{4,0},{5,1},{6,2},{7,3},{0,4},{1,5},{2,6},{3,7},{12,8},{13,9},{14,... | collective-permute-start | bytes 368648 | tf_op jit(solution)/shard_map/ppermute | solution.py:241
  12.5 1.4 %collective-permute-start.5 = (f32[240,128]{1,0:T(8,128)S(1)}, f32[240,128]{1,0:T(8,128)S(1)}, u32[]{:S(2)}, u32[]{:S(2)}) collective-permute-start(f32[240,128]{1,0:T(8,128)S(1)} %shard_map.38.refs_2_), channel_id=1, source_target_pairs={{5,0},{4,1},{7,2},{6,3},{1,4},{0,5},{3,6},{2,7},{13,8},{12,9},{15,... | collective-permute-start | bytes 368648 | tf_op jit(solution)/shard_map/ppermute | solution.py:241
  13.9 0.5 %collective-permute-start.6 = (f32[240,128]{1,0:T(8,128)S(1)}, f32[240,128]{1,0:T(8,128)S(1)}, u32[]{:S(2)}, u32[]{:S(2)}) collective-permute-start(f32[240,128]{1,0:T(8,128)S(1)} %shard_map.38.refs_2_), channel_id=1, source_target_pairs={{1,0},{0,1},{3,2},{2,3},{5,4},{4,5},{7,6},{6,7},{9,8},{8,9},{11,10... | collective-permute-start | bytes 368648 | tf_op jit(solution)/shard_map/ppermute | solution.py:241
  14.4 0.0 copy-done
  14.4 0.0 collective-permute-start
  14.4 0.0 copy-done.1
  14.5 0.1 copy.4.scale_ref
  14.5 1.1 %collective-permute-done.refs_1_ = f32[16,160]{1,0:T(8,128)S(1)} collective-permute-done((f32[16,160]{1,0:T(8,128)S(1)}, f32[16,160]{1,0:T(8,128)S(1)}, u32[]{:S(2)}, u32[]{:S(2)}) %collective-permute-start) | collective-permute-done | bytes 10272 | tf_op jit(solution)/shard_map/ppermute | solution.py:241
  15.6 1.1 %shard_map.39 = (f32[64,160]{1,0:T(8,128)S(1)}, f32[64,160]{1,0:T(8,128)S(1)}, bf16[640,112]{1,0:T(8,128)(2,1)S(1)}, f32[16,128]{1,0:T(8,128)S(1)}) custom-call(f32[16,1]{1,0:T(8,128)S(1)} %copy.4.scale_ref, f32[16,160]{1,0:T(8,128)S(1)} %copy-done, f32[16,160]{1,0:T(8,128)S(1)} %collective-permute-done.refs_1_, f32[240,128]{1,0:T(8,128)S(1)} %shard_map.38.refs_2_), custom_call_target="tpu_custom_call" | custom-call | tf_op jit(solution)/shard_map/pallas_call | solution.py:245
  16.7 0.0 collective-permute-done.4.refs_2_
  16.8 0.8 %shard_map.40 = (f32[64,160]{1,0:T(8,128)S(1)}, f32[64,160]{1,0:T(8,128)S(1)}) custom-call(f32[16,128]{1,0:T(8,128)S(1)} %get-tuple-element.32.scale_ref, bf16[640,112]{1,0:T(8,128)(2,1)S(1)} %get-tuple-element.33.feat_ref, f32[64,160]{1,0:T(8,128)S(1)} %get-tuple-element.36.refs_0_, f32[64,160]{1,0:T(8,128)S(1)} %get-tuple-element.37.refs_1_, ...), custom_call_target="tpu_custom_call" | custom-call | tf_op jit(solution)/shard_map/pallas_call | solution.py:245
  17.5 0.7 %collective-permute-done.5.refs_1_.refs_0_ = f32[240,128]{1,0:T(8,128)S(1)} collective-permute-done((f32[240,128]{1,0:T(8,128)S(1)}, f32[240,128]{1,0:T(8,128)S(1)}, u32[]{:S(2)}, u32[]{:S(2)}) %collective-permute-start.5) | collective-permute-done | bytes 122912 | tf_op jit(solution)/shard_map/ppermute | solution.py:241
  18.3 0.5 %shard_map.41.before_ref = f32[64,160]{1,0:T(8,128)S(1)} custom-call(f32[16,128]{1,0:T(8,128)S(1)} %get-tuple-element.32.scale_ref, bf16[640,112]{1,0:T(8,128)(2,1)S(1)} %get-tuple-element.33.feat_ref, f32[64,160]{1,0:T(8,128)S(1)} %get-tuple-element.42.refs_0_, f32[240,128]{1,0:T(8,128)S(1)} %collective-permute-done.5.refs_1_.refs_0_), custom_call_target="tpu_custom_call" | custom-call | tf_op jit(solution)/shard_map/pallas_call | solution.py:245
  18.8 0.0 collective-permute-done.6.refs_0_.refs_1_
  18.8 0.5 %shard_map.42 = f32[32,160]{1,0:T(8,128)S(1)} custom-call(f32[16,128]{1,0:T(8,128)S(1)} %get-tuple-element.32.scale_ref, bf16[640,112]{1,0:T(8,128)(2,1)S(1)} %get-tuple-element.33.feat_ref, f32[64,160]{1,0:T(8,128)S(1)} %shard_map.41.before_ref, f32[240,128]{1,0:T(8,128)S(1)} %collective-permute-done.6.refs_0_.refs_1_), custom_call_target="tpu_custom_call" | custom-call | tf_op jit(solution)/shard_map/pallas_call | solution.py:245
  19.3 0.0 collective-permute-start.7
  19.3 0.7 %shard_map.43 = f32[32,160]{1,0:T(8,128)S(1)} custom-call(f32[16,128]{1,0:T(8,128)S(1)} %get-tuple-element.32.scale_ref, bf16[640,112]{1,0:T(8,128)(2,1)S(1)} %get-tuple-element.33.feat_ref, f32[64,160]{1,0:T(8,128)S(1)} %get-tuple-element.47.before_ref, f32[240,128]{1,0:T(8,128)S(1)} %collective-permute-done.5.refs_1_.refs_0_, ...), custom_call_target="tpu_custom_call" | custom-call | tf_op jit(solution)/shard_map/pallas_call | solution.py:245
  20.1 0.5 %collective-permute-done.7 = f32[32,160]{1,0:T(8,128)S(1)} collective-permute-done((f32[32,160]{1,0:T(8,128)S(1)}, f32[32,160]{1,0:T(8,128)S(1)}, u32[]{:S(2)}, u32[]{:S(2)}) %collective-permute-start.7) | collective-permute-done | bytes 20512 | tf_op jit(solution)/shard_map/ppermute | solution.py:303
  20.6 0.6 %add.3 = f32[32,160]{1,0:T(8,128)} add(f32[32,160]{1,0:T(8,128)S(1)} %shard_map.43, f32[32,160]{1,0:T(8,128)S(1)} %collective-permute-done.7) | non-fusion elementwise | flops 5120 | bytes 61440 | tf_op jit(solution)/shard_map/add | solution.py:303
Async XLA Ops:
  0.8 13.6 %copy-start = (f32[16,160]{1,0:T(8,128)S(1)}, f32[16,160]{1,0:T(8,128)}, u32[]{:S(2)}) copy-start(f32[16,160]{1,0:T(8,128)} %refs_0_.1) | copy-start | bytes 30724
  0.8 7.0 %collective-permute-start.1 = (f32[64,128]{1,0:T(8,128)S(1)}, f32[64,128]{1,0:T(8,128)S(1)}, u32[]{:S(2)}, u32[]{:S(2)}) collective-permute-start(f32[64,128]{1,0:T(8,128)S(1)} %shard_map.37.refs_0_), channel_id=1, source_target_pairs={{24,0},{25,1},{26,2},{27,3},{28,4},{29,5},{30,6},{31,7},{16,8},{17... | collective-permute-start | bytes 98312 | tf_op jit(solution)/shard_map/ppermute | solution.py:241
  5.9 4.8 %collective-permute-start.2 = (f32[64,128]{1,0:T(8,128)S(1)}, f32[64,128]{1,0:T(8,128)S(1)}, u32[]{:S(2)}, u32[]{:S(2)}) collective-permute-start(f32[64,128]{1,0:T(8,128)S(1)} %shard_map.37.refs_0_), channel_id=1, source_target_pairs={{16,0},{17,1},{18,2},{19,3},{20,4},{21,5},{22,6},{23,7},{24,8},{25... | collective-permute-start | bytes 98312 | tf_op jit(solution)/shard_map/ppermute | solution.py:241
  5.9 4.8 %collective-permute-start.3 = (f32[64,128]{1,0:T(8,128)S(1)}, f32[64,128]{1,0:T(8,128)S(1)}, u32[]{:S(2)}, u32[]{:S(2)}) collective-permute-start(f32[64,128]{1,0:T(8,128)S(1)} %shard_map.37.refs_0_), channel_id=1, source_target_pairs={{8,0},{9,1},{10,2},{11,3},{12,4},{13,5},{14,6},{15,7},{0,8},{1,9},... | collective-permute-start | bytes 98312 | tf_op jit(solution)/shard_map/ppermute | solution.py:241
  10.9 3.6 %copy-start.1 = (f32[16]{0:T(128)S(1)}, f32[16]{0:T(128)}, u32[]{:S(2)}) copy-start(f32[16]{0:T(128)} %param.5) | copy-start | bytes 196
  10.9 5.9 %collective-permute-start.4 = (f32[240,128]{1,0:T(8,128)S(1)}, f32[240,128]{1,0:T(8,128)S(1)}, u32[]{:S(2)}, u32[]{:S(2)}) collective-permute-start(f32[240,128]{1,0:T(8,128)S(1)} %shard_map.38.refs_2_), channel_id=1, source_target_pairs={{4,0},{5,1},{6,2},{7,3},{0,4},{1,5},{2,6},{3,7},{12,8},{13,9},{14,... | collective-permute-start | bytes 368648 | tf_op jit(solution)/shard_map/ppermute | solution.py:241
  12.5 5.8 %collective-permute-start.5 = (f32[240,128]{1,0:T(8,128)S(1)}, f32[240,128]{1,0:T(8,128)S(1)}, u32[]{:S(2)}, u32[]{:S(2)}) collective-permute-start(f32[240,128]{1,0:T(8,128)S(1)} %shard_map.38.refs_2_), channel_id=1, source_target_pairs={{5,0},{4,1},{7,2},{6,3},{1,4},{0,5},{3,6},{2,7},{13,8},{12,9},{15,... | collective-permute-start | bytes 368648 | tf_op jit(solution)/shard_map/ppermute | solution.py:241
  13.9 4.9 %collective-permute-start.6 = (f32[240,128]{1,0:T(8,128)S(1)}, f32[240,128]{1,0:T(8,128)S(1)}, u32[]{:S(2)}, u32[]{:S(2)}) collective-permute-start(f32[240,128]{1,0:T(8,128)S(1)} %shard_map.38.refs_2_), channel_id=1, source_target_pairs={{1,0},{0,1},{3,2},{2,3},{5,4},{4,5},{7,6},{6,7},{9,8},{8,9},{11,10... | collective-permute-start | bytes 368648 | tf_op jit(solution)/shard_map/ppermute | solution.py:241
  14.4 1.2 %collective-permute-start = (f32[16,160]{1,0:T(8,128)S(1)}, f32[16,160]{1,0:T(8,128)S(1)}, u32[]{:S(2)}, u32[]{:S(2)}) collective-permute-start(f32[16,160]{1,0:T(8,128)S(1)} %copy-done), channel_id=1, source_target_pairs={{2,0},{3,1},{0,2},{1,3},{6,4},{7,5},{4,6},{5,7},{10,8},{11,9},{8,1... | collective-permute-start | bytes 30728 | tf_op jit(solution)/shard_map/ppermute | solution.py:241
  19.3 1.2 %collective-permute-start.7 = (f32[32,160]{1,0:T(8,128)S(1)}, f32[32,160]{1,0:T(8,128)S(1)}, u32[]{:S(2)}, u32[]{:S(2)}) collective-permute-start(f32[32,160]{1,0:T(8,128)S(1)} %shard_map.42), channel_id=1, source_target_pairs={{0,2},{1,3},{2,0},{3,1},{4,6},{5,7},{6,4},{7,5},{8,10},{9,11},{10,... | collective-permute-start | bytes 61448 | tf_op jit(solution)/shard_map/ppermute | solution.py:303

commit v5 on v1

--- a/solution.py
+++ b/solution.py
@@ -263,7 +263,7 @@
     later_points, block = lax.optimization_barrier((points, block))
     blocks = [send(block, "far", k) for k in [*range(2, far), 1][: far - 1]]
     row_points = [send(later_points, "pair", k) for k in range(1, pair)]
-    blocks, row_points = lax.optimization_barrier((blocks, row_points))
+    blocks = lax.optimization_barrier(blocks)
     line = pl.pallas_call(
         functools.partial(line_kernel, count, width),
         out_shape=jax.ShapeDtypeStruct(line_shape(count, width, far), jnp.float32),

time: 21.3 us -> 21.3 us (level)
  no operation moved by 1% of the time
where the time goes in v5:
time: 21.3 us; the launch traced here: 21.1 us
  starting transfers between devices  9.21 us (43%)
  waiting for transfers between devices  6.42 us (30%)
  Pallas kernels  4.49 us (21%)
  other arithmetic  0.77 us (4%)
    ppermute x7, starting transfers between devices, send(): return lax.ppermute(item, AXES, permutation(sizes, axis, step))  9.18 us
    ppermute x7, waiting for transfers between devices, send(): return lax.ppermute(item, AXES, permutation(sizes, axis, step))  5.96 us
    pallas_call x5, Pallas kernels, call(): pl.pallas_call(body, out_shape=[jax.ShapeDtypeStruct(shape, dtype) for sh...  3.65 us
    concatenate x1, other arithmetic, per_device(): jnp.concatenate([points, vectors], axis=0)  0.77 us
    pallas_call x1, Pallas kernels, per_device(): pl.pallas_call(sum_kernel, out_shape=jax.ShapeDtypeStruct((nvec, width),...  0.62 us
    ppermute x1, waiting for transfers between devices, per_device(): others.append(lax.ppermute(part, AXES, back))  0.46 us
  transfers between devices with their start and end apart: 8, of which 5 were waited for; matrix products, arithmetic and copies ran while one was open for 0% of the time, Pallas kernels for 15%

profile of v5, /device:TPU:0, one launch (start us, length us, event | category | flops | bytes accessed | tf_op | source)
XLA Modules:
  0.0 21.1 jit_solution(10624456403022151567)
XLA Ops:
  0.0 0.8 %pad_maximum_fusion.block_ref = f32[48,160]{1,0:T(8,128)S(1)} fusion(f32[32,160]{1,0:T(8,128)} %param.4, f32[16,160]{1,0:T(8,128)} %refs_0_.1), kind=kLoop, calls=%fused_computation | loop fusion | flops 7680 | bytes 61440 | tf_op jit(solution)/shard_map/concatenate | solution.py:262
  0.8 0.1 shard_map.37.refs_0_
  0.8 0.0 copy-start
  0.8 4.0 %collective-permute-start.1 = (f32[64,128]{1,0:T(8,128)S(1)}, f32[64,128]{1,0:T(8,128)S(1)}, u32[]{:S(2)}, u32[]{:S(2)}) collective-permute-start(f32[64,128]{1,0:T(8,128)S(1)} %shard_map.37.refs_0_), channel_id=1, source_target_pairs={{16,0},{17,1},{18,2},{19,3},{20,4},{21,5},{22,6},{23,7},{24,8},{25... | collective-permute-start | bytes 98312 | tf_op jit(solution)/shard_map/ppermute | solution.py:248
  4.9 1.3 %collective-permute-start.2 = (f32[64,128]{1,0:T(8,128)S(1)}, f32[64,128]{1,0:T(8,128)S(1)}, u32[]{:S(2)}, u32[]{:S(2)}) collective-permute-start(f32[64,128]{1,0:T(8,128)S(1)} %shard_map.37.refs_0_), channel_id=1, source_target_pairs={{24,0},{25,1},{26,2},{27,3},{28,4},{29,5},{30,6},{31,7},{16,8},{17... | collective-permute-start | bytes 98312 | tf_op jit(solution)/shard_map/ppermute | solution.py:248
  6.2 0.2 %collective-permute-start.3 = (f32[64,128]{1,0:T(8,128)S(1)}, f32[64,128]{1,0:T(8,128)S(1)}, u32[]{:S(2)}, u32[]{:S(2)}) collective-permute-start(f32[64,128]{1,0:T(8,128)S(1)} %shard_map.37.refs_0_), channel_id=1, source_target_pairs={{8,0},{9,1},{10,2},{11,3},{12,4},{13,5},{14,6},{15,7},{0,8},{1,9},... | collective-permute-start | bytes 98312 | tf_op jit(solution)/shard_map/ppermute | solution.py:248
  6.5 0.7 %collective-permute-done.1.refs_1_ = f32[64,128]{1,0:T(8,128)S(1)} collective-permute-done((f32[64,128]{1,0:T(8,128)S(1)}, f32[64,128]{1,0:T(8,128)S(1)}, u32[]{:S(2)}, u32[]{:S(2)}) %collective-permute-start.1) | collective-permute-done | bytes 32800 | tf_op jit(solution)/shard_map/ppermute | solution.py:248
  7.1 3.5 %collective-permute-done.2.refs_2_ = f32[64,128]{1,0:T(8,128)S(1)} collective-permute-done((f32[64,128]{1,0:T(8,128)S(1)}, f32[64,128]{1,0:T(8,128)S(1)}, u32[]{:S(2)}, u32[]{:S(2)}) %collective-permute-start.2) | collective-permute-done | bytes 32800 | tf_op jit(solution)/shard_map/ppermute | solution.py:248
  10.6 0.0 collective-permute-done.3.refs_3_
  10.6 0.1 shard_map.38.refs_2_
  10.8 0.0 copy-start.1
  10.8 1.6 %collective-permute-start.4 = (f32[240,128]{1,0:T(8,128)S(1)}, f32[240,128]{1,0:T(8,128)S(1)}, u32[]{:S(2)}, u32[]{:S(2)}) collective-permute-start(f32[240,128]{1,0:T(8,128)S(1)} %shard_map.38.refs_2_), channel_id=1, source_target_pairs={{4,0},{5,1},{6,2},{7,3},{0,4},{1,5},{2,6},{3,7},{12,8},{13,9},{14,... | collective-permute-start | bytes 368648 | tf_op jit(solution)/shard_map/ppermute | solution.py:248
  12.4 1.4 %collective-permute-start.5 = (f32[240,128]{1,0:T(8,128)S(1)}, f32[240,128]{1,0:T(8,128)S(1)}, u32[]{:S(2)}, u32[]{:S(2)}) collective-permute-start(f32[240,128]{1,0:T(8,128)S(1)} %shard_map.38.refs_2_), channel_id=1, source_target_pairs={{5,0},{4,1},{7,2},{6,3},{1,4},{0,5},{3,6},{2,7},{13,8},{12,9},{15,... | collective-permute-start | bytes 368648 | tf_op jit(solution)/shard_map/ppermute | solution.py:248
  13.8 0.5 %collective-permute-start.6 = (f32[240,128]{1,0:T(8,128)S(1)}, f32[240,128]{1,0:T(8,128)S(1)}, u32[]{:S(2)}, u32[]{:S(2)}) collective-permute-start(f32[240,128]{1,0:T(8,128)S(1)} %shard_map.38.refs_2_), channel_id=1, source_target_pairs={{1,0},{0,1},{3,2},{2,3},{5,4},{4,5},{7,6},{6,7},{9,8},{8,9},{11,10... | collective-permute-start | bytes 368648 | tf_op jit(solution)/shard_map/ppermute | solution.py:248
  14.3 0.0 copy-done
  14.3 0.0 collective-permute-start
  14.3 0.0 copy-done.1
  14.3 0.1 copy.4.scale_ref
  14.4 1.1 %collective-permute-done.refs_1_ = f32[16,160]{1,0:T(8,128)S(1)} collective-permute-done((f32[16,160]{1,0:T(8,128)S(1)}, f32[16,160]{1,0:T(8,128)S(1)}, u32[]{:S(2)}, u32[]{:S(2)}) %collective-permute-start) | collective-permute-done | bytes 10272 | tf_op jit(solution)/shard_map/ppermute | solution.py:248
  15.5 1.1 %shard_map.39 = (f32[64,160]{1,0:T(8,128)S(1)}, f32[64,160]{1,0:T(8,128)S(1)}, bf16[640,112]{1,0:T(8,128)(2,1)S(1)}, f32[16,128]{1,0:T(8,128)S(1)}) custom-call(f32[16,1]{1,0:T(8,128)S(1)} %copy.4.scale_ref, f32[16,160]{1,0:T(8,128)S(1)} %copy-done, f32[16,160]{1,0:T(8,128)S(1)} %collective-permute-done.refs_1_, f32[240,128]{1,0:T(8,128)S(1)} %shard_map.38.refs_2_), custom_call_target="tpu_custom_call" | custom-call | tf_op jit(solution)/shard_map/pallas_call | solution.py:252
  16.6 0.0 collective-permute-done.4.refs_2_
  16.6 0.8 %shard_map.40 = (f32[64,160]{1,0:T(8,128)S(1)}, f32[64,160]{1,0:T(8,128)S(1)}) custom-call(f32[16,128]{1,0:T(8,128)S(1)} %get-tuple-element.32.scale_ref, bf16[640,112]{1,0:T(8,128)(2,1)S(1)} %get-tuple-element.33.feat_ref, f32[64,160]{1,0:T(8,128)S(1)} %get-tuple-element.36.refs_0_, f32[64,160]{1,0:T(8,128)S(1)} %get-tuple-element.37.refs_1_, ...), custom_call_target="tpu_custom_call" | custom-call | tf_op jit(solution)/shard_map/pallas_call | solution.py:252
  17.4 0.7 %collective-permute-done.5.refs_1_.refs_0_ = f32[240,128]{1,0:T(8,128)S(1)} collective-permute-done((f32[240,128]{1,0:T(8,128)S(1)}, f32[240,128]{1,0:T(8,128)S(1)}, u32[]{:S(2)}, u32[]{:S(2)}) %collective-permute-start.5) | collective-permute-done | bytes 122912 | tf_op jit(solution)/shard_map/ppermute | solution.py:248
  18.1 0.5 %shard_map.41.before_ref = f32[64,160]{1,0:T(8,128)S(1)} custom-call(f32[16,128]{1,0:T(8,128)S(1)} %get-tuple-element.32.scale_ref, bf16[640,112]{1,0:T(8,128)(2,1)S(1)} %get-tuple-element.33.feat_ref, f32[64,160]{1,0:T(8,128)S(1)} %get-tuple-element.42.refs_0_, f32[240,128]{1,0:T(8,128)S(1)} %collective-permute-done.5.refs_1_.refs_0_), custom_call_target="tpu_custom_call" | custom-call | tf_op jit(solution)/shard_map/pallas_call | solution.py:252
  18.7 0.0 collective-permute-done.6.refs_0_.refs_1_
  18.7 0.5 %shard_map.42 = f32[32,160]{1,0:T(8,128)S(1)} custom-call(f32[16,128]{1,0:T(8,128)S(1)} %get-tuple-element.32.scale_ref, bf16[640,112]{1,0:T(8,128)(2,1)S(1)} %get-tuple-element.33.feat_ref, f32[64,160]{1,0:T(8,128)S(1)} %shard_map.41.before_ref, f32[240,128]{1,0:T(8,128)S(1)} %collective-permute-done.6.refs_0_.refs_1_), custom_call_target="tpu_custom_call" | custom-call | tf_op jit(solution)/shard_map/pallas_call | solution.py:252
  19.2 0.0 collective-permute-start.7
  19.2 0.7 %shard_map.43.refs_0_ = f32[32,160]{1,0:T(8,128)S(1)} custom-call(f32[16,128]{1,0:T(8,128)S(1)} %get-tuple-element.32.scale_ref, bf16[640,112]{1,0:T(8,128)(2,1)S(1)} %get-tuple-element.33.feat_ref, f32[64,160]{1,0:T(8,128)S(1)} %get-tuple-element.47.before_ref, f32[240,128]{1,0:T(8,128)S(1)} %collective-permute-done.5.refs_1_.refs_0_, ...), custom_call_target="tpu_custom_call" | custom-call | tf_op jit(solution)/shard_map/pallas_call | solution.py:252
  20.0 0.5 %collective-permute-done.7.refs_1_ = f32[32,160]{1,0:T(8,128)S(1)} collective-permute-done((f32[32,160]{1,0:T(8,128)S(1)}, f32[32,160]{1,0:T(8,128)S(1)}, u32[]{:S(2)}, u32[]{:S(2)}) %collective-permute-start.7) | collective-permute-done | bytes 20512 | tf_op jit(solution)/shard_map/ppermute | solution.py:311
  20.4 0.6 %shard_map.44 = f32[32,160]{1,0:T(8,128)} custom-call(f32[32,160]{1,0:T(8,128)S(1)} %shard_map.43.refs_0_, f32[32,160]{1,0:T(8,128)S(1)} %collective-permute-done.7.refs_1_), custom_call_target="tpu_custom_call" | custom-call | tf_op jit(solution)/shard_map/pallas_call | solution.py:312
Async XLA Ops:
  0.8 13.5 %copy-start = (f32[16,160]{1,0:T(8,128)S(1)}, f32[16,160]{1,0:T(8,128)}, u32[]{:S(2)}) copy-start(f32[16,160]{1,0:T(8,128)} %refs_0_.1) | copy-start | bytes 30724
  0.8 6.3 %collective-permute-start.1 = (f32[64,128]{1,0:T(8,128)S(1)}, f32[64,128]{1,0:T(8,128)S(1)}, u32[]{:S(2)}, u32[]{:S(2)}) collective-permute-start(f32[64,128]{1,0:T(8,128)S(1)} %shard_map.37.refs_0_), channel_id=1, source_target_pairs={{16,0},{17,1},{18,2},{19,3},{20,4},{21,5},{22,6},{23,7},{24,8},{25... | collective-permute-start | bytes 98312 | tf_op jit(solution)/shard_map/ppermute | solution.py:248
  4.9 5.7 %collective-permute-start.2 = (f32[64,128]{1,0:T(8,128)S(1)}, f32[64,128]{1,0:T(8,128)S(1)}, u32[]{:S(2)}, u32[]{:S(2)}) collective-permute-start(f32[64,128]{1,0:T(8,128)S(1)} %shard_map.37.refs_0_), channel_id=1, source_target_pairs={{24,0},{25,1},{26,2},{27,3},{28,4},{29,5},{30,6},{31,7},{16,8},{17... | collective-permute-start | bytes 98312 | tf_op jit(solution)/shard_map/ppermute | solution.py:248
  6.2 4.4 %collective-permute-start.3 = (f32[64,128]{1,0:T(8,128)S(1)}, f32[64,128]{1,0:T(8,128)S(1)}, u32[]{:S(2)}, u32[]{:S(2)}) collective-permute-start(f32[64,128]{1,0:T(8,128)S(1)} %shard_map.37.refs_0_), channel_id=1, source_target_pairs={{8,0},{9,1},{10,2},{11,3},{12,4},{13,5},{14,6},{15,7},{0,8},{1,9},... | collective-permute-start | bytes 98312 | tf_op jit(solution)/shard_map/ppermute | solution.py:248
  10.8 3.6 %copy-start.1 = (f32[16]{0:T(128)S(1)}, f32[16]{0:T(128)}, u32[]{:S(2)}) copy-start(f32[16]{0:T(128)} %param.5) | copy-start | bytes 196
  10.8 5.9 %collective-permute-start.4 = (f32[240,128]{1,0:T(8,128)S(1)}, f32[240,128]{1,0:T(8,128)S(1)}, u32[]{:S(2)}, u32[]{:S(2)}) collective-permute-start(f32[240,128]{1,0:T(8,128)S(1)} %shard_map.38.refs_2_), channel_id=1, source_target_pairs={{4,0},{5,1},{6,2},{7,3},{0,4},{1,5},{2,6},{3,7},{12,8},{13,9},{14,... | collective-permute-start | bytes 368648 | tf_op jit(solution)/shard_map/ppermute | solution.py:248
  12.4 5.8 %collective-permute-start.5 = (f32[240,128]{1,0:T(8,128)S(1)}, f32[240,128]{1,0:T(8,128)S(1)}, u32[]{:S(2)}, u32[]{:S(2)}) collective-permute-start(f32[240,128]{1,0:T(8,128)S(1)} %shard_map.38.refs_2_), channel_id=1, source_target_pairs={{5,0},{4,1},{7,2},{6,3},{1,4},{0,5},{3,6},{2,7},{13,8},{12,9},{15,... | collective-permute-start | bytes 368648 | tf_op jit(solution)/shard_map/ppermute | solution.py:248
  13.8 4.9 %collective-permute-start.6 = (f32[240,128]{1,0:T(8,128)S(1)}, f32[240,128]{1,0:T(8,128)S(1)}, u32[]{:S(2)}, u32[]{:S(2)}) collective-permute-start(f32[240,128]{1,0:T(8,128)S(1)} %shard_map.38.refs_2_), channel_id=1, source_target_pairs={{1,0},{0,1},{3,2},{2,3},{5,4},{4,5},{7,6},{6,7},{9,8},{8,9},{11,10... | collective-permute-start | bytes 368648 | tf_op jit(solution)/shard_map/ppermute | solution.py:248
  14.3 1.2 %collective-permute-start = (f32[16,160]{1,0:T(8,128)S(1)}, f32[16,160]{1,0:T(8,128)S(1)}, u32[]{:S(2)}, u32[]{:S(2)}) collective-permute-start(f32[16,160]{1,0:T(8,128)S(1)} %copy-done), channel_id=1, source_target_pairs={{2,0},{3,1},{0,2},{1,3},{6,4},{7,5},{4,6},{5,7},{10,8},{11,9},{8,1... | collective-permute-start | bytes 30728 | tf_op jit(solution)/shard_map/ppermute | solution.py:248
  19.2 1.2 %collective-permute-start.7 = (f32[32,160]{1,0:T(8,128)S(1)}, f32[32,160]{1,0:T(8,128)S(1)}, u32[]{:S(2)}, u32[]{:S(2)}) collective-permute-start(f32[32,160]{1,0:T(8,128)S(1)} %shard_map.42), channel_id=1, source_target_pairs={{0,2},{1,3},{2,0},{3,1},{4,6},{5,7},{6,4},{7,5},{8,10},{9,11},{10,... | collective-permute-start | bytes 61448 | tf_op jit(solution)/shard_map/ppermute | solution.py:311
